TPU v7x, 32 devices: a whole 2x2x4 slice. The times are simulated.
32 devices in a mesh: batch: 8 (over z, x), fsdp: 2 (over y), seq: 2 (over core).
Axes of the slice: x: 2, y: 2, z: 4, core: 2. Of those that a mesh axis runs over, the one named last changes fastest.
Arguments:
- tokens: bfloat16 [16, 1024, 960], P(('batch', 'fsdp'), 'seq'), may hold values from -6 to 6
- attn_gain: bfloat16 [960], P('fsdp'), may hold values from 0.5 to 1.5
- w_query: bfloat16 [960, 960], P('fsdp'), may hold values from -0.25 to 0.25
- key_weight: bfloat16 [960, 320], P('fsdp'), may hold values from -0.1875 to 0.1875
- value_weight: bfloat16 [960, 320], P('fsdp'), may hold values from -0.1875 to 0.1875
- w_out: bfloat16 [960, 960], P('fsdp'), may hold values from -0.75 to 0.75
- ffn_gain: bfloat16 [960], P('fsdp'), may hold values from 0.5 to 1.5
- w_gate: bfloat16 [960, 2560], P('fsdp'), may hold values from -0.1875 to 0.1875
- w_up: bfloat16 [960, 2560], P('fsdp'), may hold values from -0.1875 to 0.1875
- w_down: bfloat16 [2560, 960], P('fsdp'), may hold values from -0.125 to 0.125
- cotangent: bfloat16 [16, 1024, 960], P(('batch', 'fsdp'), 'seq'), may hold values from -6 to 6
Outputs:
- layer_output: bfloat16 [16, 1024, 960], P(('batch', 'fsdp'), 'seq')
- grad_tokens: float32 [16, 1024, 960], P(('batch', 'fsdp'), 'seq')
- grad_attn_gain: float32 [960], P('fsdp')
- grad_query: float32 [960, 960], P('fsdp')
- grad_key: float32 [960, 320], P('fsdp')
- grad_value: float32 [960, 320], P('fsdp')
- grad_out: float32 [960, 960], P('fsdp')
- grad_ffn_gain: float32 [960], P('fsdp')
- grad_gate: float32 [960, 2560], P('fsdp')
- grad_up: float32 [960, 2560], P('fsdp')
- grad_down: float32 [2560, 960], P('fsdp')
All inputs are finite; a program needn't handle non-finite values.
Results may differ from a plain program's by a relative error of at most 0.025.
Values may be sent and summed in bfloat16 or wider, within the bound.
No kernel may reach another device: no remote copies, remote signals or barrier semaphores. Data moves between devices by JAX's collectives and lax.ppermute only.
A program may use at most 320 MiB of HBM per device.

v0:
```python
import functools
import math

import jax
import jax.numpy as jnp
from jax import lax
from jax.experimental import pallas as pl
from jax.experimental.pallas import tpu as pltpu
from jax.sharding import PartitionSpec as P

QUERY_HEADS = 15
KEY_HEADS = 5
HEAD_DIM = 64
GROUP = QUERY_HEADS // KEY_HEADS
EPSILON = 1e-05
F32 = jnp.float32
BF16 = jnp.bfloat16


def dot(left, right, left_dim, right_dim):
    return lax.dot_general(
        left, right, (((left_dim,), (right_dim,)), ((), ())), preferred_element_type=F32
    )


def spans(total, size):
    return [(start, min(size, total - start)) for start in range(0, total, size)]


COSTS = {
    "project": 6.0,
    "attend": 4.0,
    "mix": 5.5,
    "expand": 10.0,
    "expand_first": 14.0,
    "shrink": 6.5,
    "shrink_first": 8.0,
    "ffn_back": 18.0,
    "attend_back": 6.5,
    "project_back": 6.0,
    "outer": 10.0,
    "pack": 4.0,
    "both_cores": 0.0,
    "cross": 0.0,
    "last": 0.0,
    "divide": 0.0,
    "split_pair": 0.0,
    "sum": 0.0,
    "unite": 0.0,
}


LIMITS = {
    "project": 12,
    "attend": 14,
    "mix": 12,
    "expand": 24,
    "expand_first": 34,
    "shrink": 22,
    "shrink_first": 34,
    "ffn_back": 40,
    "attend_back": 16,
    "project_back": 16,
    "outer": 26,
    "pack": 20,
    "both_cores": 12,
    "cross": 10,
    "last": 12,
    "divide": 10,
    "split_pair": 16,
    "sum": 6,
    "unite": 14,
}


def call(kernel, name, grid, in_specs, out_specs, out_shape, scratch=(), cost=None):
    if cost is None:
        cost = COSTS[name] * 0.45 * (grid[0] if name.startswith("attend") else 1)
    cost = int(cost * 1e9) + 1
    options = dict(
        name=name,
        out_shape=out_shape,
        compiler_params=pltpu.CompilerParams(vmem_limit_bytes=LIMITS[name] * 1024 * 1024),
        cost_estimate=pl.CostEstimate(flops=cost, bytes_accessed=1, transcendentals=0),
    )
    if name in ("project", "mix", "project_back", "pack", "both_cores", "cross", "last", "divide", "sum", "unite", "split_pair"):
        memory = pl.BlockSpec(memory_space=pltpu.VMEM)
        return pl.pallas_call(
            kernel,
            in_specs=[pl.BlockSpec(memory_space=pltpu.SMEM)] + [memory] * len(in_specs),
            out_specs=[memory] * len(out_specs),
            scratch_shapes=list(scratch),
            **options,
        )
    return pl.pallas_call(
        kernel,
        grid_spec=pltpu.PrefetchScalarGridSpec(
            num_scalar_prefetch=1,
            grid=grid,
            in_specs=in_specs,
            out_specs=out_specs,
            scratch_shapes=list(scratch),
        ),
        **options,
    )


def whole(shape):
    return pl.BlockSpec(shape, lambda *_: (0,) * len(shape))


def shaped(shape, dtype):
    return jax.ShapeDtypeStruct(shape, dtype)


def scale_of(values):
    return lax.rsqrt(jnp.mean(values * values, 0, keepdims=True) + EPSILON)


def norm_back(values, gain, incoming):
    scales = scale_of(values)
    weighted = gain * incoming
    inner = jnp.mean(values * weighted, 0, keepdims=True)
    grad = scales * weighted - values * (scales * scales * scales * inner)
    return grad, jnp.sum(incoming * values * scales, 1, keepdims=True)


def rotate(values, cosine, sine):
    half = HEAD_DIM // 2
    first, second = values[:half], values[half:]
    return first * cosine - second * sine, second * cosine + first * sine


def project_kernel(
    info, x, gain, q_weight, k_own, k_oth, v_own, v_oth, cosine, sine, normed, out
):
    width = x.shape[0]
    half = width // 2
    values = x[...].astype(F32)
    normed[...] = (values * scale_of(values) * gain[...]).astype(BF16)
    own = normed[pl.ds(pl.multiple_of(info[0] * half, half), half), :]
    oth = normed[pl.ds(pl.multiple_of((1 - info[0]) * half, half), half), :]
    cos, sin = cosine[...], sine[...]
    hd = HEAD_DIM

    def turned(rows, base, factor):
        for head in range(rows.shape[0] // hd):
            first, second = rotate(rows[head * hd : (head + 1) * hd], cos, sin)
            at = base + head * hd
            out[at : at + hd // 2, :] = (first * factor).astype(BF16)
            out[at + hd // 2 : at + hd, :] = (second * factor).astype(BF16)

    q_width = q_weight.shape[1]
    turned(dot(q_weight[...], normed[...], 0, 0), 0, hd**-0.5)
    kv = k_own.shape[0]
    turned(dot(k_own[...], own, 1, 0) + dot(k_oth[...], oth, 1, 0), q_width, 1.0)
    rows = dot(v_own[...], own, 1, 0) + dot(v_oth[...], oth, 1, 0)
    out[q_width + kv : q_width + 2 * kv, :] = rows.astype(BF16)


def project(info, x, gain, weights, tables, cost=None):
    width, rows = x.shape
    q, k, v = weights
    total = q.shape[1] + 2 * k[0].shape[0]
    operands = (x, gain, q, *k, *v, *tables)
    return call(
        project_kernel,
        "project",
        (1,),
        [whole(item.shape) for item in operands],
        [whole((width, rows)), whole((total, rows))],
        [shaped((width, rows), BF16), shaped((total, rows), BF16)],
        cost=cost,
    )(info, *operands)


def scores_of(keys, queries, masked):
    scores = dot(keys, queries, 1, 0)
    if not masked:
        return scores
    key_row = lax.broadcasted_iota(jnp.int32, scores.shape, 0)
    query_row = lax.broadcasted_iota(jnp.int32, scores.shape, 1)
    return jnp.where(key_row <= query_row, scores, -1e30)


def attend_kernel(
    info, q, k_own, v_own, k_past, v_past, out, lse, keys_own, keys_past, peak, total, mixed
):
    rows = q.shape[1]
    block = min(256, rows)
    hd = HEAD_DIM
    groups = [(group, slice(group * hd, (group + 1) * hd)) for group in range(GROUP)]
    keys_own[...] = k_own[...].T

    @pl.loop(0, info[1])
    def _(device):
        keys_past[device] = k_past[device].T

    for start in range(0, rows, block):
        for group, head in groups:
            scores = scores_of(keys_own[start : start + block, :], q[head, start:], True)
            fresh = jnp.max(scores, 0, keepdims=True)
            if start > 0:
                fresh = jnp.maximum(fresh, peak[group : group + 1, start:])
            peak[group : group + 1, start:] = fresh

    @pl.loop(0, info[1])
    def _(device):
        for group, head in groups:
            scores = scores_of(keys_past[device], q[head, :], False)
            peak[group : group + 1, :] = jnp.maximum(
                peak[group : group + 1, :], jnp.max(scores, 0, keepdims=True)
            )

    def add(group, head, keys, values, start, masked, first):
        scores = scores_of(keys, q[head, start:], masked)
        exponent = jnp.exp(scores - peak[group : group + 1, start:])
        sums = jnp.sum(exponent, 0, keepdims=True)
        product = dot(values, exponent.astype(BF16), 1, 0)
        if first:
            total[group : group + 1, :] = sums
            mixed[head, :] = product
        else:
            total[group : group + 1, start:] += sums
            mixed[head, start:] += product

    for start in range(0, rows, block):
        part = slice(start, start + block)
        for group, head in groups:
            add(group, head, keys_own[part, :], v_own[:, part], start, True, start == 0)

    @pl.loop(0, info[1])
    def _(device):
        for group, head in groups:
            add(group, head, keys_past[device], v_past[device], 0, False, False)

    for group, head in groups:
        sums = total[group : group + 1, :]
        out[head, :] = (mixed[head, :] / sums).astype(BF16)
        lse[0, group : group + 1, :] = peak[group : group + 1, :] + jnp.log(sums)


def attention_specs(rows, past, base):
    hd = HEAD_DIM
    return [
        pl.BlockSpec((GROUP * hd, rows), lambda h, info: (base + h, 0)),
        pl.BlockSpec((hd, rows), lambda h, info: (QUERY_HEADS + base + h, 0)),
        pl.BlockSpec((hd, rows), lambda h, info: (QUERY_HEADS + KEY_HEADS + base + h, 0)),
        pl.BlockSpec((past, hd, rows), lambda h, info: (0, base + h, 0)),
        pl.BlockSpec((past, hd, rows), lambda h, info: (0, KEY_HEADS + base + h, 0)),
    ]


def attend(info, qkv, past, base, heads):
    rows = qkv.shape[1]
    count = past.shape[0]
    group = GROUP * HEAD_DIM
    return call(
        attend_kernel,
        "attend",
        (heads,),
        attention_specs(rows, count, base),
        [
            pl.BlockSpec((group, rows), lambda h, info: (h, 0)),
            pl.BlockSpec((1, 8, rows), lambda h, info: (h, 0, 0)),
        ],
        [shaped((heads * group, rows), BF16), shaped((heads, 8, rows), F32)],
        [
            pltpu.VMEM((rows, HEAD_DIM), BF16),
            pltpu.VMEM((count, rows, HEAD_DIM), BF16),
            pltpu.VMEM((8, rows), F32),
            pltpu.VMEM((8, rows), F32),
            pltpu.VMEM((GROUP * HEAD_DIM, rows), F32),
        ],
    )(info, qkv, qkv, qkv, past, past)


def mix_kernel(info, x, mixed, weight, gain, middle, normed):
    middle[...] = x[...].astype(F32) + dot(weight[...], mixed[...], 0, 0)
    values = middle[...]
    normed[...] = (values * scale_of(values) * gain[...]).astype(BF16)


def mix(info, x, mixed, weight, gain):
    width, rows = x.shape
    operands = (x, mixed, weight, gain)
    return call(
        mix_kernel,
        "mix",
        (1,),
        [whole(item.shape) for item in operands],
        [whole((width, rows)), whole((width, rows))],
        [shaped((width, rows), F32), shaped((width, rows), BF16)],
    )(info, *operands)


def activate(token_rows, gate_weight, up_weight, hidden, silu, slope):
    gate = dot(token_rows[...], gate_weight[...], 1, 0)
    up = dot(token_rows[...], up_weight[...], 1, 0)
    sigmoid = 0.5 * jnp.tanh(0.5 * gate) + 0.5
    active = gate * sigmoid
    hidden[...] = (active * up).astype(BF16)
    silu[...] = active.astype(BF16)
    slope[...] = (up * (sigmoid + active * (1.0 - sigmoid))).astype(BF16)


def expand_kernel(info, normed, gate_weight, up_weight, hidden, silu, slope, token_rows):
    @pl.when(pl.program_id(0) == 0)
    def _():
        token_rows[...] = normed[...].T

    activate(token_rows, gate_weight, up_weight, hidden, silu, slope)


def expand(info, normed, gate, up):
    width, rows = normed.shape
    ff = gate.shape[1]
    tile = ff // 5
    weight = pl.BlockSpec((width, tile), lambda t, info: (0, t))
    result = pl.BlockSpec((rows, tile), lambda t, info: (0, t))
    return call(
        expand_kernel,
        "expand",
        (ff // tile,),
        [whole((width, rows)), weight, weight],
        [result] * 3,
        [shaped((rows, ff), BF16)] * 3,
        [pltpu.VMEM((rows, width), BF16)],
    )(info, normed, gate, up)


def expand_first_kernel(info, normed, *refs):
    gate_parts, up_parts = refs[:5], refs[5:10]
    hidden, silu, slope, gate_weight, up_weight, token_rows = refs[10:]
    step = pl.program_id(0)
    steps = pl.num_programs(0)

    @pl.when(step == 0)
    def _():
        token_rows[...] = normed[...].T

    for (own, *pieces), target in ((gate_parts, gate_weight), (up_parts, up_weight)):
        half, quarter = own.shape[0], pieces[0].shape[0]
        target[pl.ds(pl.multiple_of(info[0] * half, half), half), :] = own[...]
        other = (1 - info[0]) * half
        near = pl.ds(pl.multiple_of(other + info[3] * quarter, quarter), quarter)
        far = pl.ds(pl.multiple_of(other + (1 - info[3]) * quarter, quarter), quarter)

        @pl.when(step < steps // 2)
        def _():
            target[near, :] = pieces[0][...]
            target[far, :] = pieces[1][...]

        @pl.when(step >= steps // 2)
        def _():
            target[near, :] = pieces[2][...]
            target[far, :] = pieces[3][...]

    activate(token_rows, gate_weight, up_weight, hidden, silu, slope)


def expand_first(info, normed, gate, up):
    width, rows = normed.shape
    half, ff = gate[0].shape
    steps = 4
    tile = ff // steps
    quarter = half // 2

    def column(t, info):
        own = info[2] * (steps // 2) + t
        return jnp.where(t < steps // 2, own, (1 - info[2]) * (steps // 2) + t - steps // 2)

    early = pl.BlockSpec((quarter, tile), lambda t, info: (0, jnp.minimum(t, steps // 2 - 1)))
    late = pl.BlockSpec((quarter, tile), lambda t, info: (0, jnp.maximum(t - steps // 2, 0)))
    parts = [pl.BlockSpec((half, tile), lambda t, info: (0, column(t, info)))]
    parts += [early, early, late, late]
    result = pl.BlockSpec((rows, tile), lambda t, info: (0, column(t, info)))
    weight = pl.BlockSpec((width, tile), lambda t, info: (0, column(t, info)))
    return call(
        expand_first_kernel,
        "expand_first",
        (steps,),
        [whole((width, rows))] + parts * 2,
        [result] * 3 + [weight] * 2,
        [shaped((rows, ff), BF16)] * 3 + [shaped((width, ff), BF16)] * 2,
        [pltpu.VMEM((rows, width), BF16)],
    )(info, normed, *gate, *up)


def shrink_kernel(info, middle, hidden, weight, out):
    out[...] = (middle[...] + dot(weight[...], hidden[...], 1, 1)).astype(out.dtype)


def shrink(info, middle, hidden, down, dtype, cost=None):
    width, rows = middle.shape
    ff = hidden.shape[1]
    tile = width // 2
    return call(
        shrink_kernel,
        "shrink",
        (width // tile,),
        [
            pl.BlockSpec((tile, rows), lambda t, info: (t, 0)),
            whole((rows, ff)),
            pl.BlockSpec((tile, ff), lambda t, info: (t, 0)),
        ],
        [pl.BlockSpec((tile, rows), lambda t, info: (t, 0))],
        [shaped((width, rows), dtype)],
        cost=cost,
    )(info, middle, hidden, down)[0]


def shrink_first_kernel(info, middle, hidden, own, near_0, far_0, near_1, far_1, out, weight):
    half, quarter = own.shape[1], near_0.shape[0]
    weight[:, pl.ds(pl.multiple_of(info[0] * half, half), half)] = own[...]
    other = pl.ds(pl.multiple_of((1 - info[0]) * half, half), half)
    at_near = pl.ds(pl.multiple_of(info[2] * quarter, quarter), quarter)
    at_far = pl.ds(pl.multiple_of((1 - info[2]) * quarter, quarter), quarter)
    for step, near, far in ((0, near_0, far_0), (1, near_1, far_1)):

        @pl.when(pl.program_id(0) == step)
        def _():
            weight[at_near, other] = near[...]
            weight[at_far, other] = far[...]

    out[...] = middle[...] + dot(weight[...], hidden[...], 1, 1)


def shrink_first(info, middle, hidden, parts):
    width, rows = middle.shape
    ff = hidden.shape[1]
    tile = width // 2
    own, first, second, third, fourth = parts

    def row(t, info):
        return jnp.where(t == 0, info[3], 1 - info[3])

    return call(
        shrink_first_kernel,
        "shrink_first",
        (2,),
        [
            pl.BlockSpec((tile, rows), lambda t, info: (row(t, info), 0)),
            whole((rows, ff)),
            pl.BlockSpec((tile, ff // 2), lambda t, info: (row(t, info), 0)),
        ]
        + [whole(first.shape)] * 4,
        [
            pl.BlockSpec((tile, rows), lambda t, info: (row(t, info), 0)),
            pl.BlockSpec((tile, ff), lambda t, info: (row(t, info), 0)),
        ],
        [shaped((width, rows), F32), shaped((width, ff), BF16)],
    )(info, middle, hidden, own, first, third, second, fourth)


def ffn_back_kernel(
    info,
    grad,
    middle,
    gain,
    silu,
    slope,
    down,
    gate,
    up,
    out_weight,
    gate_grad,
    up_grad,
    branch,
    grad_middle,
    attn_grad,
    mixed_grad,
    gain_grad,
    branch_rows,
    total,
):
    step = pl.program_id(0)
    steps = pl.num_programs(0)

    @pl.when(step == 0)
    def _():
        branch[...] = grad[...].astype(BF16)
        branch_rows[...] = branch[...].T
        total[...] = jnp.zeros_like(total)

    incoming = dot(branch_rows[...], down[...], 1, 0)
    gate_grad[...] = (incoming * slope[...].astype(F32)).astype(BF16)
    up_grad[...] = (incoming * silu[...].astype(F32)).astype(BF16)
    total[...] += dot(gate[...], gate_grad[...], 1, 1) + dot(up[...], up_grad[...], 1, 1)

    @pl.when(step == steps - 1)
    def _():
        back, gain_sum = norm_back(middle[...], gain[...], total[...])
        gain_grad[...] = gain_sum
        result = grad[...].astype(F32) + back
        grad_middle[...] = result
        attn_grad[...] = result.astype(BF16)
        mixed_grad[...] = dot(out_weight[...], attn_grad[...], 1, 0).astype(BF16)


def ffn_back(info, grad, middle, gain, silu, slope, down, gate, up, out_weight, cost=None):
    width, rows = middle.shape
    ff = silu.shape[1]
    tile = ff // 5
    heads = out_weight.shape[0]
    token = pl.BlockSpec((rows, tile), lambda t, info: (0, t))
    weight = pl.BlockSpec((width, tile), lambda t, info: (0, t))
    return call(
        ffn_back_kernel,
        "ffn_back",
        (ff // tile,),
        [
            whole((width, rows)),
            whole((width, rows)),
            whole((width, 1)),
            token,
            token,
            weight,
            weight,
            weight,
            whole((heads, width)),
        ],
        [
            token,
            token,
            whole((width, rows)),
            whole((width, rows)),
            whole((width, rows)),
            whole((heads, rows)),
            whole((width, 1)),
        ],
        [
            shaped((rows, ff), BF16),
            shaped((rows, ff), BF16),
            shaped((width, rows), BF16),
            shaped((width, rows), F32),
            shaped((width, rows), BF16),
            shaped((heads, rows), BF16),
            shaped((width, 1), F32),
        ],
        [pltpu.VMEM((rows, width), BF16), pltpu.VMEM((width, rows), F32)],
        cost=cost,
    )(info, grad, middle, gain, silu, slope, down, gate, up, out_weight)


def attend_back_kernel(
    info,
    q,
    k_own,
    v_own,
    k_past,
    v_past,
    mixed_grad,
    mixed,
    lse,
    cosine,
    sine,
    q_grad,
    own_grad,
    past_grad,
    keys_own,
    values_own,
    keys_past,
    values_past,
    inner,
    q_sum,
):
    rows = q.shape[1]
    block = min(256, rows)
    hd = HEAD_DIM
    groups = [(group, slice(group * hd, (group + 1) * hd)) for group in range(GROUP)]
    keys_own[...] = k_own[...].T
    values_own[...] = v_own[...].T

    @pl.loop(0, info[1])
    def _(device):
        keys_past[device] = k_past[device].T
        values_past[device] = v_past[device].T

    @pl.loop(info[1], past_grad.shape[0])
    def _(device):
        past_grad[device] = jnp.zeros_like(past_grad[device])

    for group, head in groups:
        product = mixed_grad[head, :].astype(F32) * mixed[head, :].astype(F32)
        inner[group : group + 1, :] = jnp.sum(product, 0, keepdims=True)

    def step(keys, key_rows, value_rows, start, masked, first):
        key_sum = value_sum = None
        for group, head in groups:
            query, incoming = q[head, start:], mixed_grad[head, start:]
            one = slice(group, group + 1)
            probs = jnp.exp(scores_of(key_rows, query, masked) - lse[0, one, start:])
            slopes = dot(value_rows, incoming, 1, 0)
            low = (probs * (slopes - inner[one, start:])).astype(BF16)
            value_part = dot(incoming, probs.astype(BF16), 1, 1)
            key_part = dot(query, low, 1, 1)
            key_sum = key_part if key_sum is None else key_sum + key_part
            value_sum = value_part if value_sum is None else value_sum + value_part
            query_part = dot(keys, low, 1, 0)
            if first:
                q_sum[head, :] = query_part
            else:
                q_sum[head, start:] += query_part
        return key_sum, value_sum

    for start in range(0, rows, block):
        part = slice(start, start + block)
        key_sum, value_sum = step(
            k_own[:, part], keys_own[part, :], values_own[part, :], start, True, start == 0
        )
        own_grad[0, :hd, part] = key_sum
        own_grad[0, hd:, part] = value_sum

    @pl.loop(0, info[1])
    def _(device):
        key_sum, value_sum = step(
            k_past[device], keys_past[device], values_past[device], 0, False, False
        )
        past_grad[device, 0, :hd, :] = key_sum.astype(past_grad.dtype)
        past_grad[device, 0, hd:, :] = value_sum.astype(past_grad.dtype)

    cos, sin = cosine[...], -sine[...]
    for group, head in groups:
        first, second = rotate(q_sum[head, :], cos, sin)
        at = group * hd
        q_grad[at : at + hd // 2, :] = (first * hd**-0.5).astype(BF16)
        q_grad[at + hd // 2 : at + hd, :] = (second * hd**-0.5).astype(BF16)


def attend_back(info, qkv, past, mixed_grad, mixed, lse, tables, base, heads, cost=None):
    rows = qkv.shape[1]
    count = past.shape[0]
    hd = HEAD_DIM
    group = pl.BlockSpec((GROUP * hd, rows), lambda h, info: (base + h, 0))
    return call(
        attend_back_kernel,
        "attend_back",
        (heads,),
        attention_specs(rows, count, base)
        + [
            group,
            group,
            pl.BlockSpec((1, 8, rows), lambda h, info: (base + h, 0, 0)),
            whole(tables[0].shape),
            whole(tables[1].shape),
        ],
        [
            pl.BlockSpec((GROUP * hd, rows), lambda h, info: (h, 0)),
            pl.BlockSpec((1, 2 * hd, rows), lambda h, info: (h, 0, 0)),
            pl.BlockSpec((count, 1, 2 * hd, rows), lambda h, info: (0, h, 0, 0)),
        ],
        [
            shaped((heads * GROUP * hd, rows), BF16),
            shaped((heads, 2 * hd, rows), F32),
            shaped((count, heads, 2 * hd, rows), BF16 if count == 1 else F32),
        ],
        [
            pltpu.VMEM((rows, hd), BF16),
            pltpu.VMEM((rows, hd), BF16),
            pltpu.VMEM((count, rows, hd), BF16),
            pltpu.VMEM((count, rows, hd), BF16),
            pltpu.VMEM((8, rows), F32),
            pltpu.VMEM((GROUP * hd, rows), F32),
        ],
        cost=cost,
    )(info, qkv, qkv, qkv, past, past, mixed_grad, mixed, lse, *tables)


def project_back_kernel(parts, info, x, gain, grad_middle, *refs):
    q_grads, own_grads, arrived = refs[:parts], refs[parts : 2 * parts], refs[2 * parts : 3 * parts]
    (
        q_weight,
        k_own,
        k_oth,
        v_own,
        v_oth,
        cosine,
        sine,
        q_grad,
        kv_grad,
        out,
        branch,
        gain_grad,
        total,
    ) = refs[3 * parts :]
    half = x.shape[0] // 2
    hd = HEAD_DIM
    kv = KEY_HEADS * hd
    cos, sin = cosine[...], -sine[...]
    head = 0
    for piece, own, far in zip(q_grads, own_grads, arrived):
        q_grad[head * GROUP * hd : head * GROUP * hd + piece.shape[0], :] = piece[...]
        for item in range(own.shape[0]):
            both = own[item] + far[item].astype(F32)
            first, second = rotate(both[:hd], cos, sin)
            at = head * hd
            kv_grad[at : at + hd // 2, :] = first.astype(BF16)
            kv_grad[at + hd // 2 : at + hd, :] = second.astype(BF16)
            kv_grad[kv + at : kv + at + hd, :] = both[hd:].astype(BF16)
            head += 1
    total[...] = dot(q_weight[...], q_grad[...], 1, 0)
    for mine, k, v in ((info[0], k_own, v_own), (1 - info[0], k_oth, v_oth)):
        total[pl.ds(pl.multiple_of(mine * half, half), half), :] += dot(
            k[...], kv_grad[:kv, :], 0, 0
        ) + dot(v[...], kv_grad[kv:, :], 0, 0)
    back, gain_sum = norm_back(x[...].astype(F32), gain[...], total[...])
    gain_grad[...] = gain_sum
    result = grad_middle[...] + back
    out[...] = result
    branch[...] = result.astype(BF16)


def project_back(info, x, gain, grad_middle, q_grads, own_grads, arrived, weights, tables, cost=None):
    width, rows = x.shape
    q, k, v = weights
    heads = q.shape[1]
    kv = 2 * KEY_HEADS * HEAD_DIM
    operands = (x, gain, grad_middle, *q_grads, *own_grads, *arrived, q, *k, *v, *tables)
    shapes = [
        shaped((heads, rows), BF16),
        shaped((kv, rows), BF16),
        shaped((width, rows), F32),
        shaped((width, rows), BF16),
        shaped((width, 1), F32),
    ]
    return call(
        functools.partial(project_back_kernel, len(q_grads)),
        "project_back",
        (1,),
        [whole(item.shape) for item in operands],
        [whole(item.shape) for item in shapes],
        shapes,
        [pltpu.VMEM((width, rows), F32)],
        cost=cost,
    )(info, *operands)


def order_rows(info, target, sources):
    rows = sources[0].shape[1]
    size = target.shape[0] // 4
    at = 0
    for core in (1 - info[2], info[2]):
        for half in (1 - info[0], info[0]):
            start = pl.multiple_of((2 * half + core) * size, size)
            for index, source in enumerate(sources):
                target[at : at + size, index * rows : (index + 1) * rows] = source[
                    pl.ds(start, size), :
                ]
            at += size


def order_halves(info, target, sources):
    rows = sources[0].shape[1]
    size = target.shape[0] // 2
    for at, core in ((0, 1 - info[2]), (size, info[2])):
        start = pl.multiple_of(core * size, size)
        for index, source in enumerate(sources):
            target[at : at + size, index * rows : (index + 1) * rows] = source[pl.ds(start, size), :]


def outer_kernel(split_columns, info, left_a, right_a, left_b, right_b, sent, kept, left, right):
    rows = left_a.shape[1]

    @pl.when(pl.program_id(0) == 0)
    def _():
        order = order_halves if split_columns else order_rows
        order(info, left, (left_a, left_b))

    right[:rows, :] = right_a[...]
    right[rows:, :] = right_b[...]
    count, size = sent.shape[0], sent.shape[1]
    for at, out in ((0, sent), (count * size, kept)):
        product = dot(left[at : at + count * size, :], right[...], 1, 0).astype(BF16)
        for index in range(count):
            out[index] = product[index * size : (index + 1) * size]


def outer(info, parts, split_columns, cost=None):
    left_a, right_a, left_b, right_b = parts
    width, rows = left_a.shape
    columns = right_a.shape[1]
    if split_columns:
        tile = columns // 4

        def column(t, info):
            return jnp.where(t < 2, (1 - info[0]) * 2 + t, info[0] * 2 + t - 2)

        right = pl.BlockSpec((rows, tile), lambda t, info: (0, column(t, info)))
        result = pl.BlockSpec((1, width // 2, tile), lambda t, info: (t // 2, 0, t % 2))
        shape = shaped((2, width // 2, columns // 2), BF16)
    else:
        tile = columns // 5
        right = pl.BlockSpec((rows, tile), lambda t, info: (0, t))
        result = pl.BlockSpec((2, width // 4, tile), lambda t, info: (0, 0, t))
        shape = shaped((2, width // 4, columns), BF16)
    return call(
        functools.partial(outer_kernel, split_columns),
        "outer",
        (columns // tile,),
        [whole((width, rows)), right, whole((width, rows)), right],
        [result, result],
        [shape, shape],
        [pltpu.VMEM((width, 2 * rows), BF16), pltpu.VMEM((2 * rows, tile), BF16)],
        cost=cost,
    )(info, *parts)


def pack_kernel(extra, info, left_a, *refs):
    sent, kept, left, right = refs[-4:]
    refs = refs[:-4]
    gains, refs = refs[len(refs) - extra :], refs[: len(refs) - extra]
    left_b, rights_a, rights_b = refs[0], refs[1::2], refs[2::2]
    rows = left_a.shape[1]
    order_rows(info, left, (left_a, left_b))
    at = 0
    for right_a, right_b in zip(rights_a, rights_b):
        right[at : at + right_a.shape[0], :rows] = right_a[...]
        right[at : at + right_a.shape[0], rows:] = right_b[...]
        at += right_a.shape[0]
    count, size = sent.shape[0], sent.shape[1]
    for base, core, out in ((0, 1 - info[2], sent), (count * size, info[2], kept)):
        for start, span in spans(right.shape[0], 512):
            product = dot(left[base : base + count * size, :], right[start : start + span, :], 1, 1)
            for index in range(count):
                out[index, :, start : start + span] = product[
                    index * size : (index + 1) * size
                ].astype(BF16)
        for index, half in enumerate((1 - info[0], info[0])):
            part = pl.ds(pl.multiple_of((2 * half + core) * size, size), size)
            for number in range(extra // 2):
                term = gains[2 * number][part, :] + gains[2 * number + 1][part, :]
                out[index, :, at + number : at + number + 1] = term.astype(BF16)
            if extra:
                out[index, :, at + extra // 2 :] = jnp.zeros((size, extra // 2), BF16)


def pack(info, left_a, left_b, rights, gains=(), cost=None):
    width, rows = left_a.shape
    columns = sum(item.shape[0] for item in rights[::2])
    operands = (left_a, left_b, *rights, *gains)
    shape = shaped((2, width // 4, columns + len(gains)), BF16)
    return call(
        functools.partial(pack_kernel, len(gains)),
        "pack",
        (1,),
        [whole(item.shape) for item in operands],
        [whole(shape.shape)] * 2,
        [shape, shape],
        [pltpu.VMEM((width, 2 * rows), BF16), pltpu.VMEM((columns, 2 * rows), BF16)],
        cost=cost,
    )(info, *operands)


def last_kernel(info, held, query, key, value, gains):
    width, narrow = query.shape[1], key.shape[0]
    values = held[...].astype(F32)
    query[...] = values[:, :width]
    key[...] = values[:, width : width + narrow].T
    value[...] = values[:, width + narrow : width + 2 * narrow].T
    gains[...] = values[:, width + 2 * narrow :]


def last(info, held, width, narrow):
    rows, columns = held.shape
    shapes = [
        shaped((rows, width), F32),
        shaped((narrow, rows), F32),
        shaped((narrow, rows), F32),
        shaped((rows, columns - width - 2 * narrow), F32),
    ]
    return call(last_kernel, "last", (1,), [None], [None] * 4, shapes)(info, held)


def column_split(columns):
    return columns // 2 // 128 * 128


def both_cores_kernel(info, *refs):
    pairs = list(zip(refs[:-4:2], refs[1:-4:2]))
    over_y, keep_y, over_x, keep_x = refs[-4:]
    half = over_x.shape[1]
    for index, out in ((0, over_y), (1, keep_y)):
        at_y = at_x = 0
        for kept, arrived in pairs:
            total = kept[index].astype(F32) + arrived[index].astype(F32)
            split = column_split(total.shape[1])
            out[:, at_y : at_y + split] = total[:, :split].astype(BF16)
            low, top = total[:half, split:], total[half:, split:]
            end = at_x + total.shape[1] - split
            keep_x[index, :, at_x:end] = jnp.where(info[3] == 0, low, top).astype(BF16)
            over_x[index, :, at_x:end] = jnp.where(info[3] == 0, top, low).astype(BF16)
            at_y, at_x = at_y + split, end
        if at_x < keep_x.shape[2]:
            rest = jnp.zeros((half, keep_x.shape[2] - at_x), BF16)
            keep_x[index, :, at_x:] = rest
            over_x[index, :, at_x:] = rest


def both_cores(info, pairs):
    rows = pairs[0][0].shape[1]
    columns = [kept.shape[2] for kept, _ in pairs]
    split = sum(column_split(item) for item in columns)
    rest = sum(columns) - split
    if len(pairs) > 1:
        rest = -(-(split + rest) // 512) * 512 - split
    first = shaped((rows, split), BF16)
    second = shaped((2, rows // 2, rest), BF16)
    shapes = [first, first, second, second]
    operands = [item for pair in pairs for item in pair]
    return call(both_cores_kernel, "both_cores", (1,), [None] * len(operands), [None] * 4, shapes)(
        info, *operands
    )


def split_pair_kernel(info, held, first, second):
    a, b = column_split(first.shape[1]), column_split(second.shape[1])
    values = held[...]
    first[:, :a] = values[:, :a].astype(F32)
    second[:, :b] = values[:, a : a + b].astype(F32)
    rest = a + b + first.shape[1] - a
    first[:, a:] = values[:, a + b : rest].astype(F32)
    second[:, b:] = values[:, rest : rest + second.shape[1] - b].astype(F32)


def split_pair(info, held, first, second):
    shapes = [shaped((held.shape[0], first), F32), shaped((held.shape[0], second), F32)]
    return call(split_pair_kernel, "split_pair", (1,), [None], [None] * 2, shapes)(info, held)


def cross_kernel(info, keep_y, from_y, keep_x, from_x, over_x, over_y, kept):
    split, half = over_x.shape[1], over_x.shape[0]
    total = keep_y[...].astype(F32) + from_y[...].astype(F32)
    low, top = total[:half], total[half:]
    over_x[...] = jnp.where(info[3] == 0, top, low).astype(BF16)
    kept[:, :split] = jnp.where(info[3] == 0, low, top).astype(BF16)
    over_y[...] = (keep_x[0].astype(F32) + from_x[0].astype(F32)).astype(BF16)
    kept[:, split:] = (keep_x[1].astype(F32) + from_x[1].astype(F32)).astype(BF16)


def cross(info, keep_y, from_y, keep_x, from_x):
    rows, split = keep_y.shape
    rest = keep_x.shape[2]
    shapes = [
        shaped((rows // 2, split), BF16),
        shaped((rows // 2, rest), BF16),
        shaped((rows // 2, split + rest), BF16),
    ]
    return call(cross_kernel, "cross", (1,), [None] * 4, [None] * 3, shapes)(
        info, keep_y, from_y, keep_x, from_x
    )


def chosen(values, number):
    result = values[0]
    for index in range(1, len(values)):
        result = jnp.where(number == index, values[index], result)
    return result


def cut_up(values, dim, count):
    size = values.shape[dim] // count
    if dim == 0:
        return [values[index * size : (index + 1) * size] for index in range(count)]
    return [values[:, index * size : (index + 1) * size] for index in range(count)]


def divide_kernel(dim, info, kept, from_x, from_y, *outs):
    split = from_x.shape[1]
    total = kept[...].astype(F32)
    total = jnp.concatenate(
        [total[:, :split] + from_x[...].astype(F32), total[:, split:] + from_y[...].astype(F32)], 1
    )
    parts = cut_up(total, dim, 4)
    for mask, out in enumerate(outs):
        order = [parts[index ^ mask] for index in range(4)]
        out[...] = chosen(order, info[4]).astype(BF16)


def divide(info, kept, from_x, from_y, dim):
    rows, columns = kept.shape
    shape = (rows // 4, columns) if dim == 0 else (rows, columns // 4)
    return call(
        functools.partial(divide_kernel, dim),
        "divide",
        (1,),
        [None] * 3,
        [None] * 4,
        [shaped(shape, BF16)] * 4,
    )(info, kept, from_x, from_y)


def sum_kernel(info, *refs):
    total = refs[0][...].astype(F32)
    for item in refs[1:-1]:
        total = total + item[...].astype(F32)
    refs[-1][...] = total.astype(BF16)


def sum_all(info, *parts):
    shape = shaped(parts[0].shape, BF16)
    return call(sum_kernel, "sum", (1,), [None] * len(parts), [None], [shape])(info, *parts)[0]


def unite_kernel(dim, place, info, *refs):
    values, out = [item[...].astype(F32) for item in refs[:-1]], refs[-1]
    number = info[place]
    ordered = [
        chosen([values[index ^ other] for other in range(len(values))], number)
        for index in range(len(values))
    ]
    out[...] = jnp.concatenate(ordered, dim).astype(out.dtype)


def unite(info, parts, dim, place, dtype):
    shape = list(parts[0].shape)
    shape[dim] *= len(parts)
    return call(
        functools.partial(unite_kernel, dim, place),
        "unite",
        (1,),
        [None] * len(parts),
        [None],
        [shaped(tuple(shape), dtype)],
    )(info, *parts)[0]


def swap(values, axis, bit):
    size = lax.axis_size(axis)
    return lax.ppermute(values, axis, [(i, i ^ bit) for i in range(size)])


def bits_of(axis):
    size = lax.axis_size(axis)
    assert size & (size - 1) == 0
    return [1 << i for i in range(size.bit_length() - 1)]


def high(axis, bit):
    return (lax.axis_index(axis) // bit) % 2


def halves(values, dim, which):
    half = values.shape[dim] // 2
    return lax.dynamic_slice_in_dim(values, which * half, half, dim)


def joined(mine, other, dim, which):
    return jnp.where(
        which == 0,
        jnp.concatenate([mine, other], dim),
        jnp.concatenate([other, mine], dim),
    )


def tied(values, others):
    return lax.optimization_barrier((values, others))[0]


def from_pieces(own, pieces, mine, core, low_batch):
    near = joined(pieces[0], pieces[2], 0, core)
    far = joined(pieces[1], pieces[3], 0, core)
    return joined(own, joined(near, far, 0, low_batch), 0, mine)


def split_dim(shape, parts):
    if shape[0] % (8 * parts) == 0:
        return 0
    if shape[1] % (128 * parts) == 0:
        return 1
    return 0 if shape[0] % parts == 0 else 1


class Order:
    def __init__(self, token):
        self.token = token

    def __call__(self, *values):
        self.token, *values = lax.optimization_barrier((self.token, *values))
        return values[0] if len(values) == 1 else values


def quarters(values, dim, number):
    quarter = values.shape[dim] // 4
    return lax.dynamic_slice_in_dim(values, number * quarter, quarter, dim)


class Chain:
    def __init__(self, order, pair, beside=()):
        self.order, self.pair, self.beside = order, pair, beside
        self.steps = [self.core, self.first, self.second]
        self.shares = [("seq", (1,), 0), ("batch", (1,), 0)]
        exchanges = [("seq", (bit,)) for bit in bits_of("seq")[1:]]
        bits = bits_of("batch")[1:]
        self.plain = not exchanges and len(bits) == 2
        while bits:
            exchanges.append(("batch", bits[:2]))
            bits = bits[2:]
        self.steps += [functools.partial(self.add, *item) for item in exchanges]
        self.steps += [self.share] * (2 + len(exchanges))
        self.waiting = None

    result_type = F32

    def send(self):
        self.waiting = self.steps.pop(0)()

    def core(self):
        away, kept = self.pair

        def finish(arrived):
            self.parts = both_cores(self.order.token, [(kept, arrived), *self.beside])

        return [swap(self.order(away), "seq", 1)], finish

    def first(self):
        over_y, keep_y, over_x, keep_x = self.parts
        over_y, over_x = self.order(over_y, over_x)

        def finish(from_y, from_x):
            self.parts = cross(self.order.token, keep_y, from_y, keep_x, from_x)

        return [swap(over_y, "fsdp", 1), swap(over_x, "batch", 1)], finish

    def second(self):
        over_x, over_y, kept = self.parts
        over_x, over_y = self.order(over_x, over_y)

        def finish(from_x, from_y):
            if self.plain:
                self.dim = split_dim(kept.shape, 4)
                self.held = divide(self.order.token, kept, from_x, from_y, self.dim)
                return
            arrived = jnp.concatenate([from_x, from_y], 1)
            self.held = (kept.astype(F32) + arrived.astype(F32)).astype(BF16)

        return [swap(over_x, "batch", 1), swap(over_y, "fsdp", 1)], finish

    def add(self, axis, bits):
        held = self.held
        if self.plain:
            own, *parts = held
            parts = self.order(*parts)
            arrived = [
                swap(part, axis, bits[0] * (mask & 1) + bits[1] * (mask >> 1))
                for mask, part in zip((1, 2, 3), parts)
            ]
            self.shares.append((axis, bits, self.dim))

            def finish(*values):
                self.held = sum_all(self.order.token, own, *values)

            return arrived, finish
        dim = split_dim(held.shape, 2 * len(bits))
        take = halves if len(bits) == 1 else quarters
        number = sum(high(axis, bit) << index for index, bit in enumerate(bits))
        masks = range(1, 1 << len(bits))
        parts = self.order(*[take(held, dim, number ^ mask) for mask in masks])
        parts = parts if len(bits) > 1 else [parts]
        arrived = [
            swap(part, axis, sum(bit for index, bit in enumerate(bits) if mask >> index & 1))
            for mask, part in zip(masks, parts)
        ]
        self.shares.append((axis, bits, dim))

        def finish(*values):
            total = take(held, dim, number).astype(F32)
            for item in values:
                total = total + item.astype(F32)
            self.held = total.astype(BF16)

        return arrived, finish

    def share(self):
        axis, bits, dim = self.shares.pop()
        held = self.order(self.held)
        masks = range(1, 1 << len(bits))
        arrived = [
            swap(held, axis, sum(bit for index, bit in enumerate(bits) if mask >> index & 1))
            for mask in masks
        ]

        def finish(*values):
            low = high(axis, bits[0])
            if self.plain:
                place = 4 if len(bits) == 2 else 3 if axis == "batch" else 2
                dtype = BF16 if self.shares else self.result_type
                self.held = unite(self.order.token, (held, *values), dim, place, dtype)
                return
            if len(bits) == 1:
                self.held = joined(held, values[0], dim, low)
                return
            near, far = joined(held, values[0], dim, low), joined(values[1], values[2], dim, low)
            self.held = joined(near, far, dim, high(axis, bits[1]))

        return arrived, finish

    def result(self):
        while self.waiting or self.steps:
            if self.waiting:
                take(self)
            else:
                self.send()
        return self.held.astype(self.result_type)


def take(*chains):
    flat = [item for chain in chains for item in chain.waiting[0]]
    values = chains[0].order(*flat)
    values = list(values) if len(flat) > 1 else [values]
    for chain in chains:
        arrived, finish = chain.waiting
        chain.waiting = None
        finish(*values[: len(arrived)])
        values = values[len(arrived) :]


def per_device(
    tokens,
    attn_gain,
    w_query,
    key_weight,
    value_weight,
    w_out,
    ffn_gain,
    w_gate,
    w_up,
    w_down,
    cotangent,
):
    assert tokens.shape[0] == 1 and lax.axis_size("fsdp") == 2
    mine, spot, core = lax.axis_index("fsdp"), lax.axis_index("seq"), high("seq", 1)
    low_batch = high("batch", 1)
    devices = lax.axis_size("seq")
    deep = lax.axis_index("batch") // 2 % 4
    info = jnp.stack([mine, spot, core, low_batch, deep]).astype(jnp.int32)
    start_in = tokens[0].T
    incoming = cotangent[0].T
    width, rows = start_in.shape

    gains = jnp.stack([attn_gain, ffn_gain])
    gains = joined(gains, swap(gains, "fsdp", 1), 1, mine).astype(F32)[..., None]
    key_weight, value_weight, w_down = key_weight.T, value_weight.T, w_down.T
    def fsdp(values):
        return swap(values, "fsdp", 1)

    def pair(values):
        return swap(values, "batch", 1)

    def cores(values):
        return swap(values, "seq", 1)

    q_piece = halves(halves(w_query, 0, low_batch), 0, core)
    kv_piece = halves(jnp.where(core == 0, key_weight, value_weight), 0, low_batch)
    q_0, kv_0 = fsdp(q_piece), fsdp(kv_piece)
    out_0 = fsdp(tied(halves(halves(w_out, 0, low_batch), 0, core), (q_0, kv_0)))
    q_1, kv_1, q_2, kv_2 = pair(q_0), pair(kv_0), cores(q_0), cores(kv_0)
    gate_0 = fsdp(tied(halves(halves(w_gate, 0, low_batch), 1, core), out_0))
    q_3, kv_3 = cores(q_1), cores(kv_1)
    q_weight = from_pieces(w_query, (q_0, q_1, q_2, q_3), mine, core, low_batch)
    held = joined(kv_0, kv_1, 0, low_batch)
    other = joined(kv_2, kv_3, 0, low_batch)
    k_oth, v_oth = jnp.where(core == 0, held, other), jnp.where(core == 0, other, held)
    qkv_weights = (q_weight, (key_weight, k_oth), (value_weight, v_oth))

    positions = (spot * rows + jnp.arange(rows, dtype=jnp.int32)).astype(F32)
    frequency = jnp.exp(
        jnp.arange(HEAD_DIM // 2, dtype=F32) * (-2.0 * math.log(10000.0) / HEAD_DIM)
    )
    angles = frequency[:, None] * positions[None, :]
    tables = (jnp.cos(angles), jnp.sin(angles))

    def gathered(qkv):
        kv = qkv[QUERY_HEADS * HEAD_DIM :]
        if devices == 2:
            return cores(kv)[None]
        return lax.all_gather(kv, "seq")

    low_normed, low_qkv = project(info, start_in, gains[0], qkv_weights, tables)
    low_past = gathered(low_qkv)
    ready = (low_qkv, gate_0)
    up_0 = fsdp(tied(halves(halves(w_up, 0, low_batch), 1, core), ready))
    down_0 = fsdp(tied(halves(halves(w_down, 0, low_batch), 0, core), ready))
    out_1, out_2 = pair(tied(out_0, (q_1, kv_1))), cores(out_0)
    gate_1, gate_2 = pair(tied(gate_0, (low_qkv, out_1))), cores(gate_0)
    out_3 = cores(out_1)
    out_weight = from_pieces(w_out, (out_0, out_1, out_2, out_3), mine, core, low_batch)
    low_mixed, low_lse = attend(info, low_qkv, tied(low_past, out_weight), 0, KEY_HEADS)
    low_mixed = tied(low_mixed, (up_0, down_0, gate_1))
    gate_3, up_1, up_2 = cores(gate_1), pair(tied(up_0, low_mixed)), cores(up_0)
    low_middle, low_normed_ffn = mix(info, start_in, low_mixed, out_weight, gains[1])
    up_3 = cores(tied(up_1, low_middle))
    down_1, down_2 = pair(tied(down_0, (up_1, low_middle))), cores(tied(down_0, low_middle))
    low_hidden, low_silu, low_slope, gate, up = expand_first(
        info,
        low_normed_ffn,
        (w_gate, gate_0, gate_1, gate_2, gate_3),
        (w_up, up_0, up_1, up_2, up_3),
    )
    down_3 = cores(tied(down_1, low_hidden))
    middle_in, down = shrink_first(
        info, low_middle, low_hidden, (w_down, down_0, down_1, down_2, down_3)
    )

    high_normed, high_qkv = project(info, middle_in, gains[0], qkv_weights, tables)
    high_past = gathered(high_qkv)
    high_mixed, high_lse = attend(info, high_qkv, high_past, 0, KEY_HEADS)
    high_middle, high_normed_ffn = mix(info, middle_in, high_mixed, out_weight, gains[1])
    high_hidden, high_silu, high_slope = expand(info, high_normed_ffn, gate, up)

    def attention_back(qkv, past, mixed_grad, mixed, lse, base, heads, cost=None):
        return attend_back(
            info, qkv, past, mixed_grad, mixed, lse, tables, base, heads, cost
        )

    def returned(past_grad):
        if devices == 2:
            return cores(past_grad[0])
        return lax.psum_scatter(past_grad, "seq", scatter_dimension=0)

    def to_input(x, grad_middle, parts, cost=None):
        return project_back(
            info, x, gains[0], grad_middle, *zip(*parts), qkv_weights, tables, cost
        )

    high_gate, high_up, high_branch, grad_middle, high_attn, mixed_grad, high_ffn_gain = ffn_back(
        info, incoming, high_middle, gains[1], high_silu, high_slope, down, gate, up, out_weight
    )
    parts = [
        attention_back(high_qkv, high_past, mixed_grad, high_mixed, high_lse, base, heads)
        for base, heads in ((0, 3), (3, 2))
    ]
    parts = [(*part[:2], returned(part[2])) for part in parts]
    high_q, high_kv, grad_between, low_branch, high_attn_gain = to_input(
        middle_in, grad_middle, parts
    )

    order = Order(tied(info, low_branch))
    down_terms = (high_branch, high_hidden, low_branch, low_hidden)
    down_g = Chain(order, outer(info, down_terms, True))
    down_g.send()
    final_out = order(shrink(info, order(high_middle), high_hidden, down, BF16))
    take(down_g)
    down_g.send()
    low_gate, low_up, _, grad_middle, low_attn, mixed_grad, low_ffn_gain = ffn_back(
        info, order(grad_between), low_middle, gains[1], low_silu, low_slope,
        down, gate, up, out_weight,
    )
    low_attn = order(low_attn)
    take(down_g)
    down_g.send()
    out_away, out_kept = pack(info, high_mixed, low_mixed, (high_attn, order(low_attn)))
    out_far = cores(order(out_away))
    gate_terms = (high_normed_ffn, high_gate, low_normed_ffn, order(low_gate))
    gate_g = Chain(order, outer(info, gate_terms, False))
    gate_g.result_type = BF16
    gate_g.send()
    take(down_g)
    down_g.send()
    gate_g.beside = ((out_kept, order(out_far)),)
    up_terms = (high_normed_ffn, high_up, low_normed_ffn, order(low_up))
    up_g = Chain(order, outer(info, up_terms, False, 14))
    up_g.send()
    take(gate_g)
    gate_g.send()
    parts = []

    def low_part(base, heads):
        mixed_now = order(mixed_grad)
        part = attention_back(low_qkv, low_past, mixed_now, low_mixed, low_lse, base, heads)
        parts.append((order(part[0]), *part[1:]))

    low_part(0, 2)
    take(up_g, gate_g, down_g)
    gate_g.send()
    up_g.send()
    down_g.send()
    low_part(2, 3)
    parts = [(*part[:2], returned(order(part[2]))) for part in parts]
    take(gate_g, up_g, down_g)
    up_g.send()
    gate_g.send()
    low_q, low_kv, grad_start, _, low_attn_gain = to_input(
        start_in, order(grad_middle), parts, 0
    )
    low_q = order(low_q)
    take(up_g, gate_g)
    gate_g.send()
    down_g.send()
    qkv_terms = (high_q, order(low_q), high_kv, low_kv)
    gain_terms = (high_attn_gain, low_attn_gain, high_ffn_gain, low_ffn_gain)
    qkv_g = Chain(order, pack(info, high_normed, low_normed, qkv_terms, gain_terms, 0))
    qkv_g.result_type = BF16
    qkv_g.send()
    take(gate_g, down_g)
    take(qkv_g)
    qkv_g.send()
    up_g.send()
    take(qkv_g, up_g)
    qkv_g.send()
    up_g.send()
    take(qkv_g, up_g)
    qkv_g.send()
    gate_g.send()
    down_g.send()
    take(qkv_g, gate_g, down_g)
    down_grad = down_g.result()
    qkv_g.send()
    up_g.send()
    gate_g.send()
    down_grad = order(down_grad)
    take(qkv_g, up_g, gate_g)
    qkv_g.send()
    up_g.send()
    take(qkv_g, up_g)
    qkv_g.send()
    gate_grad, out_grad = split_pair(
        order.token, order(gate_g.result()), w_gate.shape[1], w_out.shape[1]
    )
    up_grad = order(up_g.result())
    held = order(qkv_g.result())
    narrow = KEY_HEADS * HEAD_DIM
    query_part, key_part, value_part, gain_grads = last(order.token, held, width, narrow)
    return (
        final_out.T[None],
        grad_start.T[None],
        gain_grads[:, 0],
        query_part,
        key_part.T,
        value_part.T,
        out_grad,
        gain_grads[:, 1],
        gate_grad,
        up_grad,
        down_grad.T,
    )


def solution(mesh):
    return jax.shard_map(
        per_device,
        mesh=mesh,
        in_specs=(
            P(("batch", "fsdp"), "seq", None),
            P("fsdp"),
            P("fsdp", None),
            P("fsdp", None),
            P("fsdp", None),
            P("fsdp", None),
            P("fsdp"),
            P("fsdp", None),
            P("fsdp", None),
            P("fsdp", None),
            P(("batch", "fsdp"), "seq", None),
        ),
        out_specs=(
            P(("batch", "fsdp"), "seq", None),
            P(("batch", "fsdp"), "seq", None),
            P("fsdp"),
            P("fsdp", None),
            P("fsdp", None),
            P("fsdp", None),
            P("fsdp", None),
            P("fsdp"),
            P("fsdp", None),
            P("fsdp", None),
            P("fsdp", None),
        ),
        check_vma=False,
    )
```

profile of v0, /device:TPU:1, one launch (start us, length us, event | category | flops | bytes accessed | tf_op | source)
XLA Modules:
  0.0 484.6 jit_solution(3459285743413364459)
XLA Ops:
  44.2 18.9 %attend.2 = (bf16[960,512]{1,0:T(8,128)(2,1)S(1)}, f32[5,8,512]{2,1,0:T(8,128)S(1)}) custom-call(s32[5]{0:T(128)S(1)} %stack.32.info, bf16[1600,512]{1,0:T(8,128)(2,1)S(1)} %get-tuple-element.324.q.k_own.v_own, bf16[1600,512]{1,0:T(8,128)(2,1)S(1)} %get-tuple-element.324.q.k_own.v_own, bf16[1600,512]{1,0:T(8,128)(2,1)S(1)} %get-tuple-element.324.q.k_own.v_own, ...), custom_call_target="tpu_custom_call" | custom-call | flops 9000000512 | bytes 1 | tf_op jit(solution)/shard_map/attend/pallas_call | solution.py:258
  64.7 4.5 collective-permute-done.16.near_0
  90.8 13.1 %expand_first.1 = (bf16[512,2560]{1,0:T(8,128)(2,1)S(1)}, bf16[512,2560]{1,0:T(8,128)(2,1)S(1)}, bf16[512,2560]{1,0:T(8,128)(2,1)S(1)}, bf16[960,2560]{1,0:T(8,128)(2,1)}, bf16[960,2560]{1,0:T(8,128)(2,1)}) custom-call(s32[5]{0:T(128)S(1)} %stack.32.info, bf16[960,512]{1,0:T(8,128)(2,1)S(1)} %copy-done.72, bf16[480,2560]{1,0:T(8,128)(2,1)S(1)} %copy-done.23, ...), custom_call_target="tpu_custom_call" | custom-call | flops 6300000256 | bytes 1 | tf_op jit(solution)/shard_map/expand_first/pallas_call | solution.py:379
  119.6 19.0 %attend.3 = (bf16[960,512]{1,0:T(8,128)(2,1)S(1)}, f32[5,8,512]{2,1,0:T(8,128)S(1)}) custom-call(s32[5]{0:T(128)S(1)} %stack.32.info, bf16[1600,512]{1,0:T(8,128)(2,1)S(1)} %get-tuple-element.343.q.k_own.v_own, bf16[1600,512]{1,0:T(8,128)(2,1)S(1)} %get-tuple-element.343.q.k_own.v_own, bf16[1600,512]{1,0:T(8,128)(2,1)S(1)} %get-tuple-element.343.q.k_own.v_own, ...), custom_call_target="tpu_custom_call" | custom-call | flops 9000000512 | bytes 1 | tf_op jit(solution)/shard_map/attend/pallas_call | solution.py:258
  141.0 8.7 %expand.1 = (bf16[512,2560]{1,0:T(8,128)(2,1)S(1)}, bf16[512,2560]{1,0:T(8,128)(2,1)S(1)}, bf16[512,2560]{1,0:T(8,128)(2,1)S(1)}) custom-call(s32[5]{0:T(128)S(1)} %stack.32.info, bf16[960,512]{1,0:T(8,128)(2,1)S(1)} %get-tuple-element.346.normed.left_a, bf16[960,2560]{1,0:T(8,128)(2,1)S(1)} %bitcast.69, bf16[960,2560]{1,0:T(8,128)(2,1)S(1)} %bitcast.71), custom_call_target="tpu_custom_call" | custom-call | flops 4500000256 | bytes 1 | tf_op jit(solution)/shard_map/expand/pallas_call | solution.py:321
  154.3 16.8 %ffn_back.2 = (bf16[512,2560]{1,0:T(8,128)(2,1)S(1)}, bf16[512,2560]{1,0:T(8,128)(2,1)}, bf16[960,512]{1,0:T(8,128)(2,1)S(1)}, f32[960,512]{1,0:T(8,128)S(1)}, b...) custom-call(s32[5]{0:T(128)S(1)} %stack.32.info, bf16[960,512]{1,0:T(8,128)(2,1)S(1)} %bitcast.49, ...), custom_call_target="tpu_custom_call" | custom-call | flops 8100000256 | bytes 1 | tf_op jit(solution)/shard_map/ffn_back/pallas_call | solution.py:508
  175.2 14.6 %attend_back.4 = (bf16[576,512]{1,0:T(8,128)(2,1)S(1)}, f32[3,128,512]{2,1,0:T(8,128)S(1)}, bf16[1,3,128,512]{3,2,1,0:T(8,128)(2,1)S(1)}) custom-call(s32[5]{0:T(128)S(1)} %stack.32.info, bf16[1600,512]{1,0:T(8,128)(2,1)S(1)} %get-tuple-element.343.q.k_own.v_own, bf16[1600,512]{1,0:T(8,128)(2,1)S(1)} %get-tuple-element.343.q.k_own.v_own, ...), custom_call_target="tpu_custom_call" | custom-call | flops 8775000064 | bytes 1 | tf_op jit(solution)/shard_map/attend_back/pallas_call | solution.py:636
  189.9 9.8 %attend_back.5 = (bf16[384,512]{1,0:T(8,128)(2,1)S(1)}, f32[2,128,512]{2,1,0:T(8,128)S(1)}, bf16[1,2,128,512]{3,2,1,0:T(8,128)(2,1)S(1)}) custom-call(s32[5]{0:T(128)S(1)} %stack.32.info, bf16[1600,512]{1,0:T(8,128)(2,1)S(1)} %get-tuple-element.343.q.k_own.v_own, bf16[1600,512]{1,0:T(8,128)(2,1)S(1)} %get-tuple-element.343.q.k_own.v_own, ...), custom_call_target="tpu_custom_call" | custom-call | flops 5849999872 | bytes 1 | tf_op jit(solution)/shard_map/attend_back/pallas_call | solution.py:636
  206.4 8.7 %outer.3 = (bf16[2,480,1280]{2,1,0:T(8,128)(2,1)S(1)}, bf16[2,480,1280]{2,1,0:T(8,128)(2,1)S(1)}) custom-call(s32[5]{0:T(128)S(1)} %stack.32.info, bf16[960,512]{1,0:T(8,128)(2,1)S(1)} %copy-done.70, bf16[512,2560]{1,0:T(8,128)(2,1)S(1)} %copy-done.37, bf16[960,512]{1,0:T(8,128)(2,1)S(1)} %get-tuple-element.361.left_b, bf16[512,2560]{1,0:T(8,128)(2,1)S(1)} %copy-done.46), custom_call_target="tpu_custom_call" | custom-call | flops 4500000256 | bytes 1 | tf_op jit(solution)/shard_map/outer/pallas_call | solution.py:797
  215.3 4.5 shrink.1
  222.9 17.1 %ffn_back.3 = (bf16[512,2560]{1,0:T(8,128)(2,1)S(1)}, bf16[512,2560]{1,0:T(8,128)(2,1)}, bf16[960,512]{1,0:T(8,128)(2,1)}, f32[960,512]{1,0:T(8,128)S(1)}, bf16[...) custom-call(s32[5]{0:T(128)S(1)} %stack.32.info, ...), custom_call_target="tpu_custom_call" | custom-call | flops 8100000256 | bytes 1 | tf_op jit(solution)/shard_map/ffn_back/pallas_call | solution.py:508
  252.8 7.3 %outer.4 = (bf16[2,240,2560]{2,1,0:T(8,128)(2,1)S(1)}, bf16[2,240,2560]{2,1,0:T(8,128)(2,1)S(1)}) custom-call(s32[5]{0:T(128)S(1)} %stack.32.info, bf16[960,512]{1,0:T(8,128)(2,1)S(1)} %copy-done.68, bf16[512,2560]{1,0:T(8,128)(2,1)S(1)} %copy-done.62, bf16[960,512]{1,0:T(8,128)(2,1)S(1)} %copy-done.73, bf16[512,2560]{1,0:T(8,128)(2,1)S(1)} %copy-done.44), custom_call_target="tpu_custom_call" | custom-call | flops 4500000256 | bytes 1 | tf_op jit(solution)/shard_map/outer/pallas_call | solution.py:797
  262.0 7.3 %outer.5 = (bf16[2,240,2560]{2,1,0:T(8,128)(2,1)S(1)}, bf16[2,240,2560]{2,1,0:T(8,128)(2,1)S(1)}) custom-call(s32[5]{0:T(128)S(1)} %stack.32.info, bf16[960,512]{1,0:T(8,128)(2,1)S(1)} %copy-done.68, bf16[512,2560]{1,0:T(8,128)(2,1)S(1)} %copy-done.60, bf16[960,512]{1,0:T(8,128)(2,1)S(1)} %copy-done.74, bf16[512,2560]{1,0:T(8,128)(2,1)S(1)} %copy-done.42), custom_call_target="tpu_custom_call" | custom-call | flops 14000000000 | bytes 1 | tf_op jit(solution)/shard_map/outer/pallas_call | solution.py:797
  277.7 5.7 %collective-permute-start.41 = (bf16[60,1280]{1,0:T(8,128)(2,1)S(1)}, bf16[60,1280]{1,0:T(8,128)(2,1)S(1)}, u32[]{:S(2)}, u32[]{:S(2)}) collective-permute-start(bf16[60,1280]{1,0:T(8,128)(2,1)S(1)} %get-tuple-element.445), channel_id=1, source_target_pairs={{0,24},{4,28},{8,16},{12,20},{16,8},{20,12},{24,0},{28,4},{1,25},{... | collective-permute-start | bytes 460808 | tf_op jit(solution)/shard_map/ppermute | solution.py:1030
  283.4 10.2 %attend_back.6 = (bf16[384,512]{1,0:T(8,128)(2,1)S(1)}, f32[2,128,512]{2,1,0:T(8,128)S(1)}, bf16[1,2,128,512]{3,2,1,0:T(8,128)(2,1)S(1)}) custom-call(s32[5]{0:T(128)S(1)} %stack.32.info, bf16[1600,512]{1,0:T(8,128)(2,1)S(1)} %copy-done.22, bf16[1600,512]{1,0:T(8,128)(2,1)S(1)} %copy-done.22, bf16[1600,512]{1,0:T(8,128)(2,1)S(1)} %copy-done.22, ...), custom_call_target="tpu_custom_call" | custom-call | flops 5849999872 | bytes 1 | tf_op jit(solution)/shard_map/attend_back/pallas_call | solution.py:636
  305.7 6.2 %collective-permute-done.47.refs_2_ = bf16[60,1280]{1,0:T(8,128)(2,1)S(1)} collective-permute-done((bf16[60,1280]{1,0:T(8,128)(2,1)S(1)}, bf16[60,1280]{1,0:T(8,128)(2,1)S(1)}, u32[]{:S(2)}, u32[]{:S(2)}) %collective-permute-start.47) | collective-permute-done | bytes 153632 | tf_op jit(solution)/shard_map/ppermute | solution.py:1030
  313.8 14.6 %attend_back.7 = (bf16[576,512]{1,0:T(8,128)(2,1)S(1)}, f32[3,128,512]{2,1,0:T(8,128)S(1)}, bf16[1,3,128,512]{3,2,1,0:T(8,128)(2,1)S(1)}) custom-call(s32[5]{0:T(128)S(1)} %stack.32.info, bf16[1600,512]{1,0:T(8,128)(2,1)S(1)} %copy-done.22, bf16[1600,512]{1,0:T(8,128)(2,1)S(1)} %copy-done.22, bf16[1600,512]{1,0:T(8,128)(2,1)S(1)} %copy-done.22, ...), custom_call_target="tpu_custom_call" | custom-call | flops 8775000064 | bytes 1 | tf_op jit(solution)/shard_map/attend_back/pallas_call | solution.py:636
  336.0 5.8 %project_back.3 = (bf16[960,512]{1,0:T(8,128)(2,1)S(1)}, bf16[640,512]{1,0:T(8,128)(2,1)S(1)}, f32[960,512]{1,0:T(8,128)}, bf16[960,512]{1,0:T(8,128)(2,1)}, f32[960,1]{1,0:T(8,128)S(1)}) custom-call(s32[5]{0:T(128)S(1)} %stack.32.info, bf16[960,512]{1,0:T(8,128)(2,1)S(1)} %bitcast.47, f32[960,1]{1,0:T(8,128)S(1)} %copy.22.gain, ...), custom_call_target="tpu_custom_call" | custom-call | flops 1 | bytes 1 | tf_op jit(solution)/shard_map/project_back/pallas_call | solution.py:727
  341.8 5.0 %collective-permute-done.55.refs_3_ = bf16[120,896]{1,0:T(8,128)(2,1)S(1)} collective-permute-done((bf16[120,896]{1,0:T(8,128)(2,1)S(1)}, bf16[120,896]{1,0:T(8,128)(2,1)S(1)}, u32[]{:S(2)}, u32[]{:S(2)}) %collective-permute-start.55) | collective-permute-done | bytes 215072 | tf_op jit(solution)/shard_map/ppermute | solution.py:1030
  351.8 4.7 collective-permute-start.60
  365.3 14.5 %collective-permute-done.57.refs_2_ = bf16[120,896]{1,0:T(8,128)(2,1)S(1)} collective-permute-done((bf16[120,896]{1,0:T(8,128)(2,1)S(1)}, bf16[120,896]{1,0:T(8,128)(2,1)S(1)}, u32[]{:S(2)}, u32[]{:S(2)}) %collective-permute-start.57) | collective-permute-done | bytes 215072 | tf_op jit(solution)/shard_map/ppermute | solution.py:1030
  404.9 8.9 %collective-permute-done.69.refs_2_ = bf16[120,640]{1,0:T(8,128)(2,1)S(1)} collective-permute-done((bf16[120,640]{1,0:T(8,128)(2,1)S(1)}, bf16[120,640]{1,0:T(8,128)(2,1)S(1)}, u32[]{:S(2)}, u32[]{:S(2)}) %collective-permute-start.69) | collective-permute-done | bytes 153632 | tf_op jit(solution)/shard_map/ppermute | solution.py:1030
  427.7 10.5 %collective-permute-done.74.refs_1_ = bf16[120,3584]{1,0:T(8,128)(2,1)S(1)} collective-permute-done((bf16[120,3584]{1,0:T(8,128)(2,1)S(1)}, bf16[120,3584]{1,0:T(8,128)(2,1)S(1)}, u32[]{:S(2)}, u32[]{:S(2)}) %collective-permute-start.74) | collective-permute-done | bytes 860192 | tf_op jit(solution)/shard_map/ppermute | solution.py:1030
  459.9 9.8 %collective-permute-done.81.refs_1_ = bf16[120,1604]{1,0:T(8,128)(2,1)S(1)} collective-permute-done((bf16[120,1604]{1,0:T(8,128)(2,1)S(1)}, bf16[120,1604]{1,0:T(8,128)(2,1)S(1)}, u32[]{:S(2)}, u32[]{:S(2)}) %collective-permute-start.81) | collective-permute-done | bytes 384992 | tf_op jit(solution)/shard_map/ppermute | solution.py:1030
  (399 shorter events, 236.4 us)
Async XLA Ops:
  22.6 18.3 %collective-permute-start.14 = (bf16[240,1280]{1,0:T(8,128)(2,1)}, bf16[240,1280]{1,0:T(8,128)(2,1)S(1)}, u32[]{:S(2)}, u32[]{:S(2)}) collective-permute-start(bf16[240,1280]{1,0:T(8,128)(2,1)} %dynamic_slice.32), channel_id=1, source_target_pairs={{0,2},{2,0},{1,3},{3,1},{4,6},{6,4},{5,7},{7,5},{8,10},{10,8},{9,1... | collective-permute-start | bytes 1843208 | tf_op jit(solution)/shard_map/ppermute | solution.py:1030
  41.0 23.7 %collective-permute-start.15 = (bf16[240,1280]{1,0:T(8,128)(2,1)S(1)}, bf16[240,1280]{1,0:T(8,128)(2,1)}, u32[]{:S(2)}, u32[]{:S(2)}) collective-permute-start(bf16[240,1280]{1,0:T(8,128)(2,1)S(1)} %dynamic_slice.31), channel_id=1, source_target_pairs={{0,2},{2,0},{1,3},{3,1},{4,6},{6,4},{5,7},{7,5},{8,10},{10,8},{9,1... | collective-permute-start | bytes 1843208 | tf_op jit(solution)/shard_map/ppermute | solution.py:1030
  41.2 28.0 %collective-permute-start.16 = (bf16[240,1280]{1,0:T(8,128)(2,1)S(1)}, bf16[240,1280]{1,0:T(8,128)(2,1)S(1)}, u32[]{:S(2)}, u32[]{:S(2)}) collective-permute-start(bf16[240,1280]{1,0:T(8,128)(2,1)S(1)} %dynamic-slice_bitcast_fusion), channel_id=1, source_target_pairs={{0,2},{2,0},{1,3},{3,1},{4,6},{6,4},{5,7},{7,5},{8,10},{10,8},{9,1... | collective-permute-start | bytes 1843208 | tf_op jit(solution)/shard_map/ppermute | solution.py:1030
  42.4 26.7 %collective-permute-start.17 = (bf16[240,1280]{1,0:T(8,128)(2,1)S(1)}, bf16[240,1280]{1,0:T(8,128)(2,1)S(1)}, u32[]{:S(2)}, u32[]{:S(2)}) collective-permute-start(bf16[240,1280]{1,0:T(8,128)(2,1)S(1)} %collective-permute-done.14.refs_1_), channel_id=1, source_target_pairs={{0,4},{4,0},{8,12},{12,8},{16,20},{20,16},{24,28},{28,24},{1,5},{5... | collective-permute-start | bytes 1843208 | tf_op jit(solution)/shard_map/ppermute | solution.py:1030
  87.7 19.2 %collective-permute-start.24 = (bf16[240,1280]{1,0:T(8,128)(2,1)S(1)}, bf16[240,1280]{1,0:T(8,128)(2,1)S(1)}, u32[]{:S(2)}, u32[]{:S(2)}) collective-permute-start(bf16[240,1280]{1,0:T(8,128)(2,1)S(1)} %copy-done.32), channel_id=1, source_target_pairs={{0,4},{4,0},{8,12},{12,8},{16,20},{20,16},{24,28},{28,24},{1,5},{5... | collective-permute-start | bytes 1843208 | tf_op jit(solution)/shard_map/ppermute | solution.py:1030
  89.1 18.1 %collective-permute-start.23 = (bf16[240,1280]{1,0:T(8,128)(2,1)S(1)}, bf16[240,1280]{1,0:T(8,128)(2,1)S(1)}, u32[]{:S(2)}, u32[]{:S(2)}) collective-permute-start(bf16[240,1280]{1,0:T(8,128)(2,1)S(1)} %copy-done.32), channel_id=1, source_target_pairs={{0,1},{1,0},{2,3},{3,2},{4,5},{5,4},{6,7},{7,6},{8,9},{9,8},{10,11... | collective-permute-start | bytes 1843208 | tf_op jit(solution)/shard_map/ppermute | solution.py:1030
  221.1 21.4 %collective-permute-start.30 = (bf16[480,640]{1,0:T(8,128)(2,1)S(1)}, bf16[480,640]{1,0:T(8,128)(2,1)S(1)}, u32[]{:S(2)}, u32[]{:S(2)}) collective-permute-start(bf16[480,640]{1,0:T(8,128)(2,1)S(1)} %get-tuple-element.385), channel_id=1, source_target_pairs={{0,2},{2,0},{1,3},{3,1},{4,6},{6,4},{5,7},{7,5},{8,10},{10,8},{9,1... | collective-permute-start | bytes 1843208 | tf_op jit(solution)/shard_map/ppermute | solution.py:1030
  221.4 21.0 %collective-permute-start.31 = (bf16[2,240,640]{2,1,0:T(8,128)(2,1)S(1)}, bf16[2,240,640]{2,1,0:T(8,128)(2,1)S(1)}, u32[]{:S(2)}, u32[]{:S(2)}) collective-permute-start(bf16[2,240,640]{2,1,0:T(8,128)(2,1)S(1)} %get-tuple-element.386), channel_id=1, source_target_pairs={{0,4},{4,0},{8,12},{12,8},{16,20},{20,16},{24,28},{28,24},{1,5},{5... | collective-permute-start | bytes 1843208 | tf_op jit(solution)/shard_map/ppermute | solution.py:1030
  269.4 24.3 %collective-permute-start.36 = (bf16[2,240,2560]{2,1,0:T(8,128)(2,1)S(1)}, bf16[2,240,2560]{2,1,0:T(8,128)(2,1)S(1)}, u32[]{:S(2)}, u32[]{:S(2)}) collective-permute-start(bf16[2,240,2560]{2,1,0:T(8,128)(2,1)S(1)} %get-tuple-element.440), channel_id=1, source_target_pairs={{0,1},{1,0},{2,3},{3,2},{4,5},{5,4},{6,7},{7,6},{8,9},{9,8},{10,11... | collective-permute-start | bytes 7372808 | tf_op jit(solution)/shard_map/ppermute | solution.py:1030
  271.0 22.7 %collective-permute-start.38 = (bf16[2,120,1920]{2,1,0:T(8,128)(2,1)S(1)}, bf16[2,120,1920]{2,1,0:T(8,128)(2,1)S(1)}, u32[]{:S(2)}, u32[]{:S(2)}) collective-permute-start(bf16[2,120,1920]{2,1,0:T(8,128)(2,1)S(1)} %get-tuple-element.442), channel_id=1, source_target_pairs={{0,4},{4,0},{8,12},{12,8},{16,20},{20,16},{24,28},{28,24},{1,5},{5... | collective-permute-start | bytes 2764808 | tf_op jit(solution)/shard_map/ppermute | solution.py:1030
  272.6 21.1 %collective-permute-start.37 = (bf16[240,1664]{1,0:T(8,128)(2,1)S(1)}, bf16[240,1664]{1,0:T(8,128)(2,1)S(1)}, u32[]{:S(2)}, u32[]{:S(2)}) collective-permute-start(bf16[240,1664]{1,0:T(8,128)(2,1)S(1)} %get-tuple-element.441), channel_id=1, source_target_pairs={{0,2},{2,0},{1,3},{3,1},{4,6},{6,4},{5,7},{7,5},{8,10},{10,8},{9,1... | collective-permute-start | bytes 2396168 | tf_op jit(solution)/shard_map/ppermute | solution.py:1030
  274.2 19.4 %collective-permute-start.40 = (bf16[60,1280]{1,0:T(8,128)(2,1)S(1)}, bf16[60,1280]{1,0:T(8,128)(2,1)S(1)}, u32[]{:S(2)}, u32[]{:S(2)}) collective-permute-start(bf16[60,1280]{1,0:T(8,128)(2,1)S(1)} %get-tuple-element.444), channel_id=1, source_target_pairs={{0,16},{4,20},{8,24},{12,28},{16,0},{20,4},{24,8},{28,12},{1,17},{... | collective-permute-start | bytes 460808 | tf_op jit(solution)/shard_map/ppermute | solution.py:1030
  298.9 29.5 %collective-permute-start.46 = (bf16[60,1280]{1,0:T(8,128)(2,1)S(1)}, bf16[60,1280]{1,0:T(8,128)(2,1)S(1)}, u32[]{:S(2)}, u32[]{:S(2)}) collective-permute-start(bf16[60,1280]{1,0:T(8,128)(2,1)S(1)} %sum.4.refs_0_), channel_id=1, source_target_pairs={{0,8},{4,12},{8,0},{12,4},{16,24},{20,28},{24,16},{28,20},{1,9},{5... | collective-permute-start | bytes 460808 | tf_op jit(solution)/shard_map/ppermute | solution.py:1030
  300.2 28.3 %collective-permute-start.42 = (bf16[120,1664]{1,0:T(8,128)(2,1)S(1)}, bf16[120,1664]{1,0:T(8,128)(2,1)S(1)}, u32[]{:S(2)}, u32[]{:S(2)}) collective-permute-start(bf16[120,1664]{1,0:T(8,128)(2,1)S(1)} %get-tuple-element.472), channel_id=1, source_target_pairs={{0,4},{4,0},{8,12},{12,8},{16,20},{20,16},{24,28},{28,24},{1,5},{5... | collective-permute-start | bytes 1198088 | tf_op jit(solution)/shard_map/ppermute | solution.py:1030
  300.7 28.2 %collective-permute-start.43 = (bf16[120,1920]{1,0:T(8,128)(2,1)S(1)}, bf16[120,1920]{1,0:T(8,128)(2,1)S(1)}, u32[]{:S(2)}, u32[]{:S(2)}) collective-permute-start(bf16[120,1920]{1,0:T(8,128)(2,1)S(1)} %get-tuple-element.473), channel_id=1, source_target_pairs={{0,2},{2,0},{1,3},{3,1},{4,6},{6,4},{5,7},{7,5},{8,10},{10,8},{9,1... | collective-permute-start | bytes 1382408 | tf_op jit(solution)/shard_map/ppermute | solution.py:1030
  304.0 24.9 %collective-permute-start.44 = (bf16[240,1280]{1,0:T(8,128)(2,1)S(1)}, bf16[240,1280]{1,0:T(8,128)(2,1)S(1)}, u32[]{:S(2)}, u32[]{:S(2)}) collective-permute-start(bf16[240,1280]{1,0:T(8,128)(2,1)S(1)} %get-tuple-element.474), channel_id=1, source_target_pairs={{0,2},{2,0},{1,3},{3,1},{4,6},{6,4},{5,7},{7,5},{8,10},{10,8},{9,1... | collective-permute-start | bytes 1843208 | tf_op jit(solution)/shard_map/ppermute | solution.py:1030
  311.8 17.1 %collective-permute-start.45 = (bf16[2,120,1280]{2,1,0:T(8,128)(2,1)S(1)}, bf16[2,120,1280]{2,1,0:T(8,128)(2,1)S(1)}, u32[]{:S(2)}, u32[]{:S(2)}) collective-permute-start(bf16[2,120,1280]{2,1,0:T(8,128)(2,1)S(1)} %get-tuple-element.475), channel_id=1, source_target_pairs={{0,4},{4,0},{8,12},{12,8},{16,20},{20,16},{24,28},{28,24},{1,5},{5... | collective-permute-start | bytes 1843208 | tf_op jit(solution)/shard_map/ppermute | solution.py:1030
  351.8 28.0 %collective-permute-start.60 = (bf16[2,240,1604]{2,1,0:T(8,128)(2,1)S(1)}, bf16[2,240,1604]{2,1,0:T(8,128)(2,1)S(1)}, u32[]{:S(2)}, u32[]{:S(2)}) collective-permute-start(bf16[2,240,1604]{2,1,0:T(8,128)(2,1)S(1)} %get-tuple-element.536), channel_id=1, source_target_pairs={{0,1},{1,0},{2,3},{3,2},{4,5},{5,4},{6,7},{7,6},{8,9},{9,8},{10,11... | collective-permute-start | bytes 4619528 | tf_op jit(solution)/shard_map/ppermute | solution.py:1030
  356.5 23.3 %collective-permute-start.59 = (bf16[240,1280]{1,0:T(8,128)(2,1)S(1)}, bf16[240,1280]{1,0:T(8,128)(2,1)S(1)}, u32[]{:S(2)}, u32[]{:S(2)}) collective-permute-start(bf16[240,1280]{1,0:T(8,128)(2,1)S(1)} %unite.12.refs_0_), channel_id=1, source_target_pairs={{0,4},{4,0},{8,12},{12,8},{16,20},{20,16},{24,28},{28,24},{1,5},{5... | collective-permute-start | bytes 1843208 | tf_op jit(solution)/shard_map/ppermute | solution.py:1030
  358.6 21.2 %collective-permute-start.57 = (bf16[120,896]{1,0:T(8,128)(2,1)S(1)}, bf16[120,896]{1,0:T(8,128)(2,1)S(1)}, u32[]{:S(2)}, u32[]{:S(2)}) collective-permute-start(bf16[120,896]{1,0:T(8,128)(2,1)S(1)} %sum.5.refs_0_), channel_id=1, source_target_pairs={{0,16},{4,20},{8,24},{12,28},{16,0},{20,4},{24,8},{28,12},{1,17},{... | collective-permute-start | bytes 645128 | tf_op jit(solution)/shard_map/ppermute | solution.py:1030
  362.0 17.9 %collective-permute-start.56 = (bf16[120,896]{1,0:T(8,128)(2,1)S(1)}, bf16[120,896]{1,0:T(8,128)(2,1)S(1)}, u32[]{:S(2)}, u32[]{:S(2)}) collective-permute-start(bf16[120,896]{1,0:T(8,128)(2,1)S(1)} %sum.5.refs_0_), channel_id=1, source_target_pairs={{0,8},{4,12},{8,0},{12,4},{16,24},{20,28},{24,16},{28,20},{1,9},{5... | collective-permute-start | bytes 645128 | tf_op jit(solution)/shard_map/ppermute | solution.py:1030
  396.0 17.8 %collective-permute-start.67 = (bf16[120,836]{1,0:T(8,128)(2,1)S(1)}, bf16[120,836]{1,0:T(8,128)(2,1)S(1)}, u32[]{:S(2)}, u32[]{:S(2)}) collective-permute-start(bf16[120,836]{1,0:T(8,128)(2,1)S(1)} %get-tuple-element.569), channel_id=1, source_target_pairs={{0,2},{2,0},{1,3},{3,1},{4,6},{6,4},{5,7},{7,5},{8,10},{10,8},{9,1... | collective-permute-start | bytes 601928 | tf_op jit(solution)/shard_map/ppermute | solution.py:1030
  414.8 23.3 %collective-permute-start.75 = (bf16[480,1280]{1,0:T(8,128)(2,1)S(1)}, bf16[480,1280]{1,0:T(8,128)(2,1)S(1)}, u32[]{:S(2)}, u32[]{:S(2)}) collective-permute-start(bf16[480,1280]{1,0:T(8,128)(2,1)S(1)} %unite.14.refs_0_), channel_id=1, source_target_pairs={{0,1},{1,0},{2,3},{3,2},{4,5},{5,4},{6,7},{7,6},{8,9},{9,8},{10,11... | collective-permute-start | bytes 3686408 | tf_op jit(solution)/shard_map/ppermute | solution.py:1030
  417.5 20.7 %collective-permute-start.74 = (bf16[120,3584]{1,0:T(8,128)(2,1)S(1)}, bf16[120,3584]{1,0:T(8,128)(2,1)S(1)}, u32[]{:S(2)}, u32[]{:S(2)}) collective-permute-start(bf16[120,3584]{1,0:T(8,128)(2,1)S(1)} %unite.13.refs_0_), channel_id=1, source_target_pairs={{0,4},{4,0},{8,12},{12,8},{16,20},{20,16},{24,28},{28,24},{1,5},{5... | collective-permute-start | bytes 2580488 | tf_op jit(solution)/shard_map/ppermute | solution.py:1030
  (145 other events, 1184.3 us)
where the time goes:
time: 492 us; the launch traced here: 485 us
  Pallas kernels  239 us (49%)
  waiting for transfers between devices  95.7 us (19%)
  starting transfers between devices  95.3 us (19%)
  local copies, waits for them, and re-layouts  44 us (9%)
  other arithmetic  8.07 us (2%)
    ppermute x84, waiting for transfers between devices, swap(): return lax.ppermute(values, axis, [(i, i ^ bit) for i in range(size)])  95.7 us
    ppermute x84, starting transfers between devices, swap(): return lax.ppermute(values, axis, [(i, i ^ bit) for i in range(size)])  95.3 us
    pallas_call x4, Pallas kernels, attend_back(): call(attend_back_kernel, 'attend_back', (heads,), attention_specs(rows, c...  49.1 us
    pallas_call x2, Pallas kernels, attend(): call(attend_kernel, 'attend', (heads,), attention_specs(rows, count, base...  37.9 us
    pallas_call x2, Pallas kernels, ffn_back(): call(ffn_back_kernel, 'ffn_back', (ff // tile,), [whole((width, rows)), w...  33.9 us
    unnamed x170, local copies, waits for them, and re-layouts  33.2 us
    pallas_call x3, Pallas kernels, outer(): call(functools.partial(outer_kernel, split_columns), 'outer', (columns //...  23.3 us
    pallas_call x12, Pallas kernels, unite(): call(functools.partial(unite_kernel, dim, place), 'unite', (1,), [None] *...  15.9 us
  transfers between devices with their start and end apart: 84, of which 26 were waited for; matrix products, arithmetic and copies ran while one was open for 3% of the time, Pallas kernels for 28%

commit v1 on v0

--- a/solution.py
+++ b/solution.py
@@ -1238,8 +1238,6 @@
     incoming = cotangent[0].T
     width, rows = start_in.shape
 
-    gains = jnp.stack([attn_gain, ffn_gain])
-    gains = joined(gains, swap(gains, "fsdp", 1), 1, mine).astype(F32)[..., None]
     key_weight, value_weight, w_down = key_weight.T, value_weight.T, w_down.T
     def fsdp(values):
         return swap(values, "fsdp", 1)
@@ -1253,6 +1251,9 @@
     q_piece = halves(halves(w_query, 0, low_batch), 0, core)
     kv_piece = halves(jnp.where(core == 0, key_weight, value_weight), 0, low_batch)
     q_0, kv_0 = fsdp(q_piece), fsdp(kv_piece)
+    gains = jnp.stack([attn_gain, ffn_gain])
+    far_gains = fsdp(tied(gains, q_0))
+    gains = joined(gains, far_gains, 1, mine).astype(F32)[..., None]
     out_0 = fsdp(tied(halves(halves(w_out, 0, low_batch), 0, core), (q_0, kv_0)))
     q_1, kv_1, q_2, kv_2 = pair(q_0), pair(kv_0), cores(q_0), cores(kv_0)
     gate_0 = fsdp(tied(halves(halves(w_gate, 0, low_batch), 1, core), out_0))
@@ -1412,11 +1413,11 @@
     take(qkv_g, up_g, gate_g)
     qkv_g.send()
     up_g.send()
+    gate_grad, out_grad = order(
+        *split_pair(order.token, gate_g.result(), w_gate.shape[1], w_out.shape[1])
+    )
     take(qkv_g, up_g)
     qkv_g.send()
-    gate_grad, out_grad = split_pair(
-        order.token, order(gate_g.result()), w_gate.shape[1], w_out.shape[1]
-    )
     up_grad = order(up_g.result())
     held = order(qkv_g.result())
     narrow = KEY_HEADS * HEAD_DIM

time: 492 us -> 489 us (level)
  starting transfers between devices: 95.3 us -> 80.9 us
  waiting for transfers between devices: 95.7 us -> 108 us
    ppermute x84, starting transfers between devices: 95.3 us -> 80.9 us  [swap(): return lax.ppermute(values, axis, [(i, i ^ bit) for i in range(size)])]
    ppermute x84, waiting for transfers between devices: 95.7 us -> 108 us  [swap(): return lax.ppermute(values, axis, [(i, i ^ bit) for i in range(size)])]
  transfers between devices with their start and end apart: 84 -> 84, of which waited for: 26 -> 24; matrix products, arithmetic and copies ran while one was open for 3% -> 4% of each run, Pallas kernels for 28% -> 28%
where the time goes in v1:
time: 489 us; the launch traced here: 482 us
  Pallas kernels  239 us (49%)
  waiting for transfers between devices  108 us (22%)
  starting transfers between devices  80.9 us (17%)
  local copies, waits for them, and re-layouts  44 us (9%)
  other arithmetic  8.07 us (2%)
    ppermute x84, waiting for transfers between devices, swap(): return lax.ppermute(values, axis, [(i, i ^ bit) for i in range(size)])  108 us
    ppermute x84, starting transfers between devices, swap(): return lax.ppermute(values, axis, [(i, i ^ bit) for i in range(size)])  80.9 us
    pallas_call x4, Pallas kernels, attend_back(): call(attend_back_kernel, 'attend_back', (heads,), attention_specs(rows, c...  49.1 us
    pallas_call x2, Pallas kernels, attend(): call(attend_kernel, 'attend', (heads,), attention_specs(rows, count, base...  37.9 us
    pallas_call x2, Pallas kernels, ffn_back(): call(ffn_back_kernel, 'ffn_back', (ff // tile,), [whole((width, rows)), w...  33.9 us
    unnamed x170, local copies, waits for them, and re-layouts  33.2 us
    pallas_call x3, Pallas kernels, outer(): call(functools.partial(outer_kernel, split_columns), 'outer', (columns //...  23.3 us
    pallas_call x12, Pallas kernels, unite(): call(functools.partial(unite_kernel, dim, place), 'unite', (1,), [None] *...  15.9 us
  transfers between devices with their start and end apart: 84, of which 24 were waited for; matrix products, arithmetic and copies ran while one was open for 4% of the time, Pallas kernels for 28%

profile of v1, /device:TPU:1, one launch (start us, length us, event | category | flops | bytes accessed | tf_op | source)
XLA Modules:
  0.0 482.0 jit_solution(7593208289541243566)
XLA Ops:
  20.8 5.1 %collective-permute-done.10 = bf16[120,960]{1,0:T(8,128)(2,1)} collective-permute-done((bf16[120,960]{1,0:T(8,128)(2,1)S(1)}, bf16[120,960]{1,0:T(8,128)(2,1)}, u32[]{:S(2)}, u32[]{:S(2)}) %collective-permute-start.10) | collective-permute-done | bytes 230432 | tf_op jit(solution)/shard_map/ppermute | solution.py:1030
  45.5 18.9 %attend.2 = (bf16[960,512]{1,0:T(8,128)(2,1)S(1)}, f32[5,8,512]{2,1,0:T(8,128)S(1)}) custom-call(s32[5]{0:T(128)S(1)} %stack.32.info, bf16[1600,512]{1,0:T(8,128)(2,1)S(1)} %get-tuple-element.327.q.k_own.v_own, bf16[1600,512]{1,0:T(8,128)(2,1)S(1)} %get-tuple-element.327.q.k_own.v_own, bf16[1600,512]{1,0:T(8,128)(2,1)S(1)} %get-tuple-element.327.q.k_own.v_own, ...), custom_call_target="tpu_custom_call" | custom-call | flops 9000000512 | bytes 1 | tf_op jit(solution)/shard_map/attend/pallas_call | solution.py:258
  66.0 6.0 %collective-permute-done.16.near_0 = bf16[240,1280]{1,0:T(8,128)(2,1)S(1)} collective-permute-done((bf16[240,1280]{1,0:T(8,128)(2,1)S(1)}, bf16[240,1280]{1,0:T(8,128)(2,1)S(1)}, u32[]{:S(2)}, u32[]{:S(2)}) %collective-permute-start.16) | collective-permute-done | bytes 614432 | tf_op jit(solution)/shard_map/ppermute | solution.py:1030
  93.3 13.1 %expand_first.1 = (bf16[512,2560]{1,0:T(8,128)(2,1)S(1)}, bf16[512,2560]{1,0:T(8,128)(2,1)S(1)}, bf16[512,2560]{1,0:T(8,128)(2,1)S(1)}, bf16[960,2560]{1,0:T(8,128)(2,1)}, bf16[960,2560]{1,0:T(8,128)(2,1)}) custom-call(s32[5]{0:T(128)S(1)} %stack.32.info, bf16[960,512]{1,0:T(8,128)(2,1)S(1)} %copy-done.72, bf16[480,2560]{1,0:T(8,128)(2,1)S(1)} %copy-done.23, ...), custom_call_target="tpu_custom_call" | custom-call | flops 6300000256 | bytes 1 | tf_op jit(solution)/shard_map/expand_first/pallas_call | solution.py:379
  122.1 19.0 %attend.3 = (bf16[960,512]{1,0:T(8,128)(2,1)S(1)}, f32[5,8,512]{2,1,0:T(8,128)S(1)}) custom-call(s32[5]{0:T(128)S(1)} %stack.32.info, bf16[1600,512]{1,0:T(8,128)(2,1)S(1)} %get-tuple-element.346.q.k_own.v_own, bf16[1600,512]{1,0:T(8,128)(2,1)S(1)} %get-tuple-element.346.q.k_own.v_own, bf16[1600,512]{1,0:T(8,128)(2,1)S(1)} %get-tuple-element.346.q.k_own.v_own, ...), custom_call_target="tpu_custom_call" | custom-call | flops 9000000512 | bytes 1 | tf_op jit(solution)/shard_map/attend/pallas_call | solution.py:258
  143.6 8.7 %expand.1 = (bf16[512,2560]{1,0:T(8,128)(2,1)S(1)}, bf16[512,2560]{1,0:T(8,128)(2,1)S(1)}, bf16[512,2560]{1,0:T(8,128)(2,1)S(1)}) custom-call(s32[5]{0:T(128)S(1)} %stack.32.info, bf16[960,512]{1,0:T(8,128)(2,1)S(1)} %get-tuple-element.349.normed.left_a, bf16[960,2560]{1,0:T(8,128)(2,1)S(1)} %bitcast.69, bf16[960,2560]{1,0:T(8,128)(2,1)S(1)} %bitcast.71), custom_call_target="tpu_custom_call" | custom-call | flops 4500000256 | bytes 1 | tf_op jit(solution)/shard_map/expand/pallas_call | solution.py:321
  156.8 16.8 %ffn_back.2 = (bf16[512,2560]{1,0:T(8,128)(2,1)S(1)}, bf16[512,2560]{1,0:T(8,128)(2,1)}, bf16[960,512]{1,0:T(8,128)(2,1)S(1)}, f32[960,512]{1,0:T(8,128)S(1)}, b...) custom-call(s32[5]{0:T(128)S(1)} %stack.32.info, bf16[960,512]{1,0:T(8,128)(2,1)S(1)} %bitcast.49, ...), custom_call_target="tpu_custom_call" | custom-call | flops 8100000256 | bytes 1 | tf_op jit(solution)/shard_map/ffn_back/pallas_call | solution.py:508
  177.7 14.6 %attend_back.4 = (bf16[576,512]{1,0:T(8,128)(2,1)S(1)}, f32[3,128,512]{2,1,0:T(8,128)S(1)}, bf16[1,3,128,512]{3,2,1,0:T(8,128)(2,1)S(1)}) custom-call(s32[5]{0:T(128)S(1)} %stack.32.info, bf16[1600,512]{1,0:T(8,128)(2,1)S(1)} %get-tuple-element.346.q.k_own.v_own, bf16[1600,512]{1,0:T(8,128)(2,1)S(1)} %get-tuple-element.346.q.k_own.v_own, ...), custom_call_target="tpu_custom_call" | custom-call | flops 8775000064 | bytes 1 | tf_op jit(solution)/shard_map/attend_back/pallas_call | solution.py:636
  192.4 9.8 %attend_back.5 = (bf16[384,512]{1,0:T(8,128)(2,1)S(1)}, f32[2,128,512]{2,1,0:T(8,128)S(1)}, bf16[1,2,128,512]{3,2,1,0:T(8,128)(2,1)S(1)}) custom-call(s32[5]{0:T(128)S(1)} %stack.32.info, bf16[1600,512]{1,0:T(8,128)(2,1)S(1)} %get-tuple-element.346.q.k_own.v_own, bf16[1600,512]{1,0:T(8,128)(2,1)S(1)} %get-tuple-element.346.q.k_own.v_own, ...), custom_call_target="tpu_custom_call" | custom-call | flops 5849999872 | bytes 1 | tf_op jit(solution)/shard_map/attend_back/pallas_call | solution.py:636
  208.9 8.7 %outer.3 = (bf16[2,480,1280]{2,1,0:T(8,128)(2,1)S(1)}, bf16[2,480,1280]{2,1,0:T(8,128)(2,1)S(1)}) custom-call(s32[5]{0:T(128)S(1)} %stack.32.info, bf16[960,512]{1,0:T(8,128)(2,1)S(1)} %copy-done.70, bf16[512,2560]{1,0:T(8,128)(2,1)S(1)} %copy-done.37, bf16[960,512]{1,0:T(8,128)(2,1)S(1)} %get-tuple-element.364.left_b, bf16[512,2560]{1,0:T(8,128)(2,1)S(1)} %copy-done.46), custom_call_target="tpu_custom_call" | custom-call | flops 4500000256 | bytes 1 | tf_op jit(solution)/shard_map/outer/pallas_call | solution.py:797
  217.8 4.5 shrink.1
  224.0 17.1 %ffn_back.3 = (bf16[512,2560]{1,0:T(8,128)(2,1)S(1)}, bf16[512,2560]{1,0:T(8,128)(2,1)}, bf16[960,512]{1,0:T(8,128)(2,1)}, f32[960,512]{1,0:T(8,128)S(1)}, bf16[...) custom-call(s32[5]{0:T(128)S(1)} %stack.32.info, ...), custom_call_target="tpu_custom_call" | custom-call | flops 8100000256 | bytes 1 | tf_op jit(solution)/shard_map/ffn_back/pallas_call | solution.py:508
  255.3 7.3 %outer.4 = (bf16[2,240,2560]{2,1,0:T(8,128)(2,1)S(1)}, bf16[2,240,2560]{2,1,0:T(8,128)(2,1)S(1)}) custom-call(s32[5]{0:T(128)S(1)} %stack.32.info, bf16[960,512]{1,0:T(8,128)(2,1)S(1)} %copy-done.68, bf16[512,2560]{1,0:T(8,128)(2,1)S(1)} %copy-done.62, bf16[960,512]{1,0:T(8,128)(2,1)S(1)} %copy-done.73, bf16[512,2560]{1,0:T(8,128)(2,1)S(1)} %copy-done.44), custom_call_target="tpu_custom_call" | custom-call | flops 4500000256 | bytes 1 | tf_op jit(solution)/shard_map/outer/pallas_call | solution.py:797
  264.6 7.3 %outer.5 = (bf16[2,240,2560]{2,1,0:T(8,128)(2,1)S(1)}, bf16[2,240,2560]{2,1,0:T(8,128)(2,1)S(1)}) custom-call(s32[5]{0:T(128)S(1)} %stack.32.info, bf16[960,512]{1,0:T(8,128)(2,1)S(1)} %copy-done.68, bf16[512,2560]{1,0:T(8,128)(2,1)S(1)} %copy-done.60, bf16[960,512]{1,0:T(8,128)(2,1)S(1)} %copy-done.74, bf16[512,2560]{1,0:T(8,128)(2,1)S(1)} %copy-done.42), custom_call_target="tpu_custom_call" | custom-call | flops 14000000000 | bytes 1 | tf_op jit(solution)/shard_map/outer/pallas_call | solution.py:797
  285.0 10.2 %attend_back.6 = (bf16[384,512]{1,0:T(8,128)(2,1)S(1)}, f32[2,128,512]{2,1,0:T(8,128)S(1)}, bf16[1,2,128,512]{3,2,1,0:T(8,128)(2,1)S(1)}) custom-call(s32[5]{0:T(128)S(1)} %stack.32.info, bf16[1600,512]{1,0:T(8,128)(2,1)S(1)} %copy-done.22, bf16[1600,512]{1,0:T(8,128)(2,1)S(1)} %copy-done.22, bf16[1600,512]{1,0:T(8,128)(2,1)S(1)} %copy-done.22, ...), custom_call_target="tpu_custom_call" | custom-call | flops 5849999872 | bytes 1 | tf_op jit(solution)/shard_map/attend_back/pallas_call | solution.py:636
  305.9 8.9 %collective-permute-done.47.refs_2_ = bf16[60,1280]{1,0:T(8,128)(2,1)S(1)} collective-permute-done((bf16[60,1280]{1,0:T(8,128)(2,1)S(1)}, bf16[60,1280]{1,0:T(8,128)(2,1)S(1)}, u32[]{:S(2)}, u32[]{:S(2)}) %collective-permute-start.47) | collective-permute-done | bytes 153632 | tf_op jit(solution)/shard_map/ppermute | solution.py:1030
  314.8 14.6 %attend_back.7 = (bf16[576,512]{1,0:T(8,128)(2,1)S(1)}, f32[3,128,512]{2,1,0:T(8,128)S(1)}, bf16[1,3,128,512]{3,2,1,0:T(8,128)(2,1)S(1)}) custom-call(s32[5]{0:T(128)S(1)} %stack.32.info, bf16[1600,512]{1,0:T(8,128)(2,1)S(1)} %copy-done.22, bf16[1600,512]{1,0:T(8,128)(2,1)S(1)} %copy-done.22, bf16[1600,512]{1,0:T(8,128)(2,1)S(1)} %copy-done.22, ...), custom_call_target="tpu_custom_call" | custom-call | flops 8775000064 | bytes 1 | tf_op jit(solution)/shard_map/attend_back/pallas_call | solution.py:636
  338.9 5.8 %project_back.3 = (bf16[960,512]{1,0:T(8,128)(2,1)S(1)}, bf16[640,512]{1,0:T(8,128)(2,1)S(1)}, f32[960,512]{1,0:T(8,128)}, bf16[960,512]{1,0:T(8,128)(2,1)}, f32[960,1]{1,0:T(8,128)S(1)}) custom-call(s32[5]{0:T(128)S(1)} %stack.32.info, bf16[960,512]{1,0:T(8,128)(2,1)S(1)} %bitcast.47, f32[960,1]{1,0:T(8,128)S(1)} %copy.22.gain, ...), custom_call_target="tpu_custom_call" | custom-call | flops 1 | bytes 1 | tf_op jit(solution)/shard_map/project_back/pallas_call | solution.py:727
  344.7 6.0 %collective-permute-done.55.refs_3_ = bf16[120,896]{1,0:T(8,128)(2,1)S(1)} collective-permute-done((bf16[120,896]{1,0:T(8,128)(2,1)S(1)}, bf16[120,896]{1,0:T(8,128)(2,1)S(1)}, u32[]{:S(2)}, u32[]{:S(2)}) %collective-permute-start.55) | collective-permute-done | bytes 215072 | tf_op jit(solution)/shard_map/ppermute | solution.py:1030
  368.0 14.5 %collective-permute-done.57.refs_2_ = bf16[120,896]{1,0:T(8,128)(2,1)S(1)} collective-permute-done((bf16[120,896]{1,0:T(8,128)(2,1)S(1)}, bf16[120,896]{1,0:T(8,128)(2,1)S(1)}, u32[]{:S(2)}, u32[]{:S(2)}) %collective-permute-start.57) | collective-permute-done | bytes 215072 | tf_op jit(solution)/shard_map/ppermute | solution.py:1030
  392.3 4.6 collective-permute-done.65.refs_3_
  407.6 8.8 %collective-permute-done.69.refs_2_ = bf16[120,640]{1,0:T(8,128)(2,1)S(1)} collective-permute-done((bf16[120,640]{1,0:T(8,128)(2,1)S(1)}, bf16[120,640]{1,0:T(8,128)(2,1)S(1)}, u32[]{:S(2)}, u32[]{:S(2)}) %collective-permute-start.69) | collective-permute-done | bytes 153632 | tf_op jit(solution)/shard_map/ppermute | solution.py:1030
  430.3 10.6 %collective-permute-done.74.refs_1_ = bf16[120,3584]{1,0:T(8,128)(2,1)S(1)} collective-permute-done((bf16[120,3584]{1,0:T(8,128)(2,1)S(1)}, bf16[120,3584]{1,0:T(8,128)(2,1)S(1)}, u32[]{:S(2)}, u32[]{:S(2)}) %collective-permute-start.74) | collective-permute-done | bytes 860192 | tf_op jit(solution)/shard_map/ppermute | solution.py:1030
  467.1 5.2 %collective-permute-done.81.refs_1_ = bf16[120,1604]{1,0:T(8,128)(2,1)S(1)} collective-permute-done((bf16[120,1604]{1,0:T(8,128)(2,1)S(1)}, bf16[120,1604]{1,0:T(8,128)(2,1)S(1)}, u32[]{:S(2)}, u32[]{:S(2)}) %collective-permute-start.81) | collective-permute-done | bytes 384992 | tf_op jit(solution)/shard_map/ppermute | solution.py:1030
  (399 shorter events, 233.9 us)
Async XLA Ops:
  43.8 22.2 %collective-permute-start.15 = (bf16[240,1280]{1,0:T(8,128)(2,1)S(1)}, bf16[240,1280]{1,0:T(8,128)(2,1)}, u32[]{:S(2)}, u32[]{:S(2)}) collective-permute-start(bf16[240,1280]{1,0:T(8,128)(2,1)S(1)} %dynamic_slice.31), channel_id=1, source_target_pairs={{0,2},{2,0},{1,3},{3,1},{4,6},{6,4},{5,7},{7,5},{8,10},{10,8},{9,1... | collective-permute-start | bytes 1843208 | tf_op jit(solution)/shard_map/ppermute | solution.py:1030
  44.0 28.0 %collective-permute-start.16 = (bf16[240,1280]{1,0:T(8,128)(2,1)S(1)}, bf16[240,1280]{1,0:T(8,128)(2,1)S(1)}, u32[]{:S(2)}, u32[]{:S(2)}) collective-permute-start(bf16[240,1280]{1,0:T(8,128)(2,1)S(1)} %dynamic-slice_bitcast_fusion), channel_id=1, source_target_pairs={{0,2},{2,0},{1,3},{3,1},{4,6},{6,4},{5,7},{7,5},{8,10},{10,8},{9,1... | collective-permute-start | bytes 1843208 | tf_op jit(solution)/shard_map/ppermute | solution.py:1030
  45.2 26.7 %collective-permute-start.17 = (bf16[240,1280]{1,0:T(8,128)(2,1)S(1)}, bf16[240,1280]{1,0:T(8,128)(2,1)S(1)}, u32[]{:S(2)}, u32[]{:S(2)}) collective-permute-start(bf16[240,1280]{1,0:T(8,128)(2,1)S(1)} %collective-permute-done.14.refs_1_), channel_id=1, source_target_pairs={{0,4},{4,0},{8,12},{12,8},{16,20},{20,16},{24,28},{28,24},{1,5},{5... | collective-permute-start | bytes 1843208 | tf_op jit(solution)/shard_map/ppermute | solution.py:1030
  90.2 19.2 %collective-permute-start.24 = (bf16[240,1280]{1,0:T(8,128)(2,1)S(1)}, bf16[240,1280]{1,0:T(8,128)(2,1)S(1)}, u32[]{:S(2)}, u32[]{:S(2)}) collective-permute-start(bf16[240,1280]{1,0:T(8,128)(2,1)S(1)} %copy-done.32), channel_id=1, source_target_pairs={{0,4},{4,0},{8,12},{12,8},{16,20},{20,16},{24,28},{28,24},{1,5},{5... | collective-permute-start | bytes 1843208 | tf_op jit(solution)/shard_map/ppermute | solution.py:1030
  90.4 19.4 %collective-permute-start.23 = (bf16[240,1280]{1,0:T(8,128)(2,1)S(1)}, bf16[240,1280]{1,0:T(8,128)(2,1)S(1)}, u32[]{:S(2)}, u32[]{:S(2)}) collective-permute-start(bf16[240,1280]{1,0:T(8,128)(2,1)S(1)} %copy-done.32), channel_id=1, source_target_pairs={{0,1},{1,0},{2,3},{3,2},{4,5},{5,4},{6,7},{7,6},{8,9},{9,8},{10,11... | collective-permute-start | bytes 1843208 | tf_op jit(solution)/shard_map/ppermute | solution.py:1030
  223.6 19.9 %collective-permute-start.30 = (bf16[480,640]{1,0:T(8,128)(2,1)S(1)}, bf16[480,640]{1,0:T(8,128)(2,1)S(1)}, u32[]{:S(2)}, u32[]{:S(2)}) collective-permute-start(bf16[480,640]{1,0:T(8,128)(2,1)S(1)} %get-tuple-element.388), channel_id=1, source_target_pairs={{0,2},{2,0},{1,3},{3,1},{4,6},{6,4},{5,7},{7,5},{8,10},{10,8},{9,1... | collective-permute-start | bytes 1843208 | tf_op jit(solution)/shard_map/ppermute | solution.py:1030
  223.7 19.9 %collective-permute-start.31 = (bf16[2,240,640]{2,1,0:T(8,128)(2,1)S(1)}, bf16[2,240,640]{2,1,0:T(8,128)(2,1)S(1)}, u32[]{:S(2)}, u32[]{:S(2)}) collective-permute-start(bf16[2,240,640]{2,1,0:T(8,128)(2,1)S(1)} %get-tuple-element.389), channel_id=1, source_target_pairs={{0,4},{4,0},{8,12},{12,8},{16,20},{20,16},{24,28},{28,24},{1,5},{5... | collective-permute-start | bytes 1843208 | tf_op jit(solution)/shard_map/ppermute | solution.py:1030
  271.9 23.4 %collective-permute-start.36 = (bf16[2,240,2560]{2,1,0:T(8,128)(2,1)S(1)}, bf16[2,240,2560]{2,1,0:T(8,128)(2,1)S(1)}, u32[]{:S(2)}, u32[]{:S(2)}) collective-permute-start(bf16[2,240,2560]{2,1,0:T(8,128)(2,1)S(1)} %get-tuple-element.443), channel_id=1, source_target_pairs={{0,1},{1,0},{2,3},{3,2},{4,5},{5,4},{6,7},{7,6},{8,9},{9,8},{10,11... | collective-permute-start | bytes 7372808 | tf_op jit(solution)/shard_map/ppermute | solution.py:1030
  273.5 21.7 %collective-permute-start.38 = (bf16[2,120,1920]{2,1,0:T(8,128)(2,1)S(1)}, bf16[2,120,1920]{2,1,0:T(8,128)(2,1)S(1)}, u32[]{:S(2)}, u32[]{:S(2)}) collective-permute-start(bf16[2,120,1920]{2,1,0:T(8,128)(2,1)S(1)} %get-tuple-element.445), channel_id=1, source_target_pairs={{0,4},{4,0},{8,12},{12,8},{16,20},{20,16},{24,28},{28,24},{1,5},{5... | collective-permute-start | bytes 2764808 | tf_op jit(solution)/shard_map/ppermute | solution.py:1030
  273.9 21.4 %collective-permute-start.37 = (bf16[240,1664]{1,0:T(8,128)(2,1)S(1)}, bf16[240,1664]{1,0:T(8,128)(2,1)S(1)}, u32[]{:S(2)}, u32[]{:S(2)}) collective-permute-start(bf16[240,1664]{1,0:T(8,128)(2,1)S(1)} %get-tuple-element.444), channel_id=1, source_target_pairs={{0,2},{2,0},{1,3},{3,1},{4,6},{6,4},{5,7},{7,5},{8,10},{10,8},{9,1... | collective-permute-start | bytes 2396168 | tf_op jit(solution)/shard_map/ppermute | solution.py:1030
  275.5 19.7 %collective-permute-start.40 = (bf16[60,1280]{1,0:T(8,128)(2,1)S(1)}, bf16[60,1280]{1,0:T(8,128)(2,1)S(1)}, u32[]{:S(2)}, u32[]{:S(2)}) collective-permute-start(bf16[60,1280]{1,0:T(8,128)(2,1)S(1)} %get-tuple-element.447), channel_id=1, source_target_pairs={{0,16},{4,20},{8,24},{12,28},{16,0},{20,4},{24,8},{28,12},{1,17},{... | collective-permute-start | bytes 460808 | tf_op jit(solution)/shard_map/ppermute | solution.py:1030
  301.4 27.9 %collective-permute-start.46 = (bf16[60,1280]{1,0:T(8,128)(2,1)S(1)}, bf16[60,1280]{1,0:T(8,128)(2,1)S(1)}, u32[]{:S(2)}, u32[]{:S(2)}) collective-permute-start(bf16[60,1280]{1,0:T(8,128)(2,1)S(1)} %sum.4.refs_0_), channel_id=1, source_target_pairs={{0,8},{4,12},{8,0},{12,4},{16,24},{20,28},{24,16},{28,20},{1,9},{5... | collective-permute-start | bytes 460808 | tf_op jit(solution)/shard_map/ppermute | solution.py:1030
  301.8 27.7 %collective-permute-start.42 = (bf16[120,1664]{1,0:T(8,128)(2,1)S(1)}, bf16[120,1664]{1,0:T(8,128)(2,1)S(1)}, u32[]{:S(2)}, u32[]{:S(2)}) collective-permute-start(bf16[120,1664]{1,0:T(8,128)(2,1)S(1)} %get-tuple-element.475), channel_id=1, source_target_pairs={{0,4},{4,0},{8,12},{12,8},{16,20},{20,16},{24,28},{28,24},{1,5},{5... | collective-permute-start | bytes 1198088 | tf_op jit(solution)/shard_map/ppermute | solution.py:1030
  303.0 27.0 %collective-permute-start.43 = (bf16[120,1920]{1,0:T(8,128)(2,1)S(1)}, bf16[120,1920]{1,0:T(8,128)(2,1)S(1)}, u32[]{:S(2)}, u32[]{:S(2)}) collective-permute-start(bf16[120,1920]{1,0:T(8,128)(2,1)S(1)} %get-tuple-element.476), channel_id=1, source_target_pairs={{0,2},{2,0},{1,3},{3,1},{4,6},{6,4},{5,7},{7,5},{8,10},{10,8},{9,1... | collective-permute-start | bytes 1382408 | tf_op jit(solution)/shard_map/ppermute | solution.py:1030
  304.7 25.3 %collective-permute-start.44 = (bf16[240,1280]{1,0:T(8,128)(2,1)S(1)}, bf16[240,1280]{1,0:T(8,128)(2,1)S(1)}, u32[]{:S(2)}, u32[]{:S(2)}) collective-permute-start(bf16[240,1280]{1,0:T(8,128)(2,1)S(1)} %get-tuple-element.477), channel_id=1, source_target_pairs={{0,2},{2,0},{1,3},{3,1},{4,6},{6,4},{5,7},{7,5},{8,10},{10,8},{9,1... | collective-permute-start | bytes 1843208 | tf_op jit(solution)/shard_map/ppermute | solution.py:1030
  330.9 19.8 %collective-permute-start.51 = (bf16[120,1280]{1,0:T(8,128)(2,1)S(1)}, bf16[120,1280]{1,0:T(8,128)(2,1)S(1)}, u32[]{:S(2)}, u32[]{:S(2)}) collective-permute-start(bf16[120,1280]{1,0:T(8,128)(2,1)S(1)} %get-tuple-element.507), channel_id=1, source_target_pairs={{0,4},{4,0},{8,12},{12,8},{16,20},{20,16},{24,28},{28,24},{1,5},{5... | collective-permute-start | bytes 921608 | tf_op jit(solution)/shard_map/ppermute | solution.py:1030
  332.4 18.2 %collective-permute-start.52 = (bf16[120,1280]{1,0:T(8,128)(2,1)S(1)}, bf16[120,1280]{1,0:T(8,128)(2,1)S(1)}, u32[]{:S(2)}, u32[]{:S(2)}) collective-permute-start(bf16[120,1280]{1,0:T(8,128)(2,1)S(1)} %get-tuple-element.508), channel_id=1, source_target_pairs={{0,2},{2,0},{1,3},{3,1},{4,6},{6,4},{5,7},{7,5},{8,10},{10,8},{9,1... | collective-permute-start | bytes 921608 | tf_op jit(solution)/shard_map/ppermute | solution.py:1030
  355.7 26.8 %collective-permute-start.60 = (bf16[2,240,1604]{2,1,0:T(8,128)(2,1)S(1)}, bf16[2,240,1604]{2,1,0:T(8,128)(2,1)S(1)}, u32[]{:S(2)}, u32[]{:S(2)}) collective-permute-start(bf16[2,240,1604]{2,1,0:T(8,128)(2,1)S(1)} %get-tuple-element.539), channel_id=1, source_target_pairs={{0,1},{1,0},{2,3},{3,2},{4,5},{5,4},{6,7},{7,6},{8,9},{9,8},{10,11... | collective-permute-start | bytes 4619528 | tf_op jit(solution)/shard_map/ppermute | solution.py:1030
  358.6 23.9 %collective-permute-start.59 = (bf16[240,1280]{1,0:T(8,128)(2,1)S(1)}, bf16[240,1280]{1,0:T(8,128)(2,1)S(1)}, u32[]{:S(2)}, u32[]{:S(2)}) collective-permute-start(bf16[240,1280]{1,0:T(8,128)(2,1)S(1)} %unite.12.refs_0_), channel_id=1, source_target_pairs={{0,4},{4,0},{8,12},{12,8},{16,20},{20,16},{24,28},{28,24},{1,5},{5... | collective-permute-start | bytes 1843208 | tf_op jit(solution)/shard_map/ppermute | solution.py:1030
  361.4 21.1 %collective-permute-start.57 = (bf16[120,896]{1,0:T(8,128)(2,1)S(1)}, bf16[120,896]{1,0:T(8,128)(2,1)S(1)}, u32[]{:S(2)}, u32[]{:S(2)}) collective-permute-start(bf16[120,896]{1,0:T(8,128)(2,1)S(1)} %sum.5.refs_0_), channel_id=1, source_target_pairs={{0,16},{4,20},{8,24},{12,28},{16,0},{20,4},{24,8},{28,12},{1,17},{... | collective-permute-start | bytes 645128 | tf_op jit(solution)/shard_map/ppermute | solution.py:1030
  363.7 18.8 %collective-permute-start.56 = (bf16[120,896]{1,0:T(8,128)(2,1)S(1)}, bf16[120,896]{1,0:T(8,128)(2,1)S(1)}, u32[]{:S(2)}, u32[]{:S(2)}) collective-permute-start(bf16[120,896]{1,0:T(8,128)(2,1)S(1)} %sum.5.refs_0_), channel_id=1, source_target_pairs={{0,8},{4,12},{8,0},{12,4},{16,24},{20,28},{24,16},{28,20},{1,9},{5... | collective-permute-start | bytes 645128 | tf_op jit(solution)/shard_map/ppermute | solution.py:1030
  397.7 18.6 %collective-permute-start.67 = (bf16[120,836]{1,0:T(8,128)(2,1)S(1)}, bf16[120,836]{1,0:T(8,128)(2,1)S(1)}, u32[]{:S(2)}, u32[]{:S(2)}) collective-permute-start(bf16[120,836]{1,0:T(8,128)(2,1)S(1)} %get-tuple-element.572), channel_id=1, source_target_pairs={{0,2},{2,0},{1,3},{3,1},{4,6},{6,4},{5,7},{7,5},{8,10},{10,8},{9,1... | collective-permute-start | bytes 601928 | tf_op jit(solution)/shard_map/ppermute | solution.py:1030
  417.4 23.5 %collective-permute-start.75 = (bf16[480,1280]{1,0:T(8,128)(2,1)S(1)}, bf16[480,1280]{1,0:T(8,128)(2,1)S(1)}, u32[]{:S(2)}, u32[]{:S(2)}) collective-permute-start(bf16[480,1280]{1,0:T(8,128)(2,1)S(1)} %unite.14.refs_0_), channel_id=1, source_target_pairs={{0,1},{1,0},{2,3},{3,2},{4,5},{5,4},{6,7},{7,6},{8,9},{9,8},{10,11... | collective-permute-start | bytes 3686408 | tf_op jit(solution)/shard_map/ppermute | solution.py:1030
  420.1 20.7 %collective-permute-start.74 = (bf16[120,3584]{1,0:T(8,128)(2,1)S(1)}, bf16[120,3584]{1,0:T(8,128)(2,1)S(1)}, u32[]{:S(2)}, u32[]{:S(2)}) collective-permute-start(bf16[120,3584]{1,0:T(8,128)(2,1)S(1)} %unite.13.refs_0_), channel_id=1, source_target_pairs={{0,4},{4,0},{8,12},{12,8},{16,20},{20,16},{24,28},{28,24},{1,5},{5... | collective-permute-start | bytes 2580488 | tf_op jit(solution)/shard_map/ppermute | solution.py:1030
  (145 other events, 1192.5 us)
